TPU v7x, 256 devices: a whole 4x4x8 slice. The times are simulated.
256 devices in a mesh: ctx: 16 (over y, x), head: 8 (over z), pipe: 2 (over core).
Axes of the slice: x: 4, y: 4, z: 8, core: 2. Of those that a mesh axis runs over, the one named last changes fastest.
Arguments:
- queries: bfloat16 [2, 2048, 8192], P('pipe', 'ctx', 'head'), may hold values from -6 to 6
- keys: bfloat16 [2, 2048, 8192], P('pipe', 'ctx', 'head'), may hold values from -6 to 6
- values: bfloat16 [2, 2048, 8192], P('pipe', 'ctx', 'head'), may hold values from -6 to 6
- gates: bfloat16 [2, 2048, 8192], P('pipe', 'ctx', 'head'), may hold values from -6 to 6
- log_decay: float32 [2, 2048, 64], P('pipe', 'ctx', 'head'), may hold values from -1 to 0
- segment_ids: int32 [2, 2048], P('pipe', 'ctx'), may hold values from 0 to 7, never falling along the last dimension, each value on 1 to 512 neighbouring positions
- norm_gain: float32 [2, 8192], P('pipe', 'head'), may hold values from 0.1 to 1.9
- out_weight: bfloat16 [2, 8192, 6144], P('pipe', 'head', 'ctx'), may hold values from -0.0625 to 0.0625
Outputs:
- handed: bfloat16 [2, 2048, 6144], P('pipe', 'ctx', 'head')
Inputs may be any that keep to these rules, and one draw needn't show every extreme that they name: `segment_ids`: along each section's tokens the ids never fall; a document has at most a quarter of 2048 tokens, and one has exactly that many.
All inputs are finite; a program needn't handle non-finite values.
Results may differ from a plain program's by a relative error of at most 0.02.
Values may be sent and summed in bfloat16 or wider, within the bound.
A program may use at most 64 MiB of HBM per device.

v0:
```python
import jax
import jax.numpy as jnp
from jax import lax
from jax.sharding import PartitionSpec as P

DH = 128


highest = lax.Precision.HIGHEST


def entering(shard, axis, combine, identity):
    count, index = (lax.axis_size(axis), lax.axis_index(axis))
    everything = jax.tree.map(
        lambda part, kind: lax.all_gather(part.astype(kind), axis),
        shard,
        (jnp.bfloat16, jnp.bfloat16, jnp.bfloat16),
    )
    start = jax.tree.map(
        lambda part, zero: jnp.broadcast_to(jnp.asarray(zero, part.dtype), part.shape),
        shard,
        identity,
    )

    def hop(k, before):
        reached = k < index
        new = combine(
            before, jax.tree.map(lambda part, own: part[k].astype(own.dtype), everything, shard)
        )
        return jax.tree.map(lambda a, b: jnp.where(reached, a, b), new, before)

    return lax.fori_loop(0, count, hop, start)


def from_behind(shard, axis, by):
    count = lax.axis_size(axis)
    return lax.ppermute(shard, axis, [(i, (i + by) % count) for i in range(count)])


def block_step(carried, pieces):
    kv_state, doc_id = carried
    query_rows, key_rows, value_rows, rate_rows, doc_rows = pieces
    length = doc_rows.shape[0]
    running = jnp.cumsum(rate_rows, axis=0)
    running_t = running.T
    causal = lax.broadcasted_iota(jnp.int32, (length, length), 0) >= lax.broadcasted_iota(
        jnp.int32, (length, length), 1
    )
    allowed = causal & (doc_rows[:, None] == doc_rows[None, :])
    log_gaps = running_t[:, :, None] - running_t[:, None, :]
    weights = jnp.where(allowed[None], jnp.exp(jnp.where(allowed[None], log_gaps, 0.0)), 0.0)
    scores = jnp.einsum("ihd,jhd->hij", query_rows, key_rows, preferred_element_type=jnp.float32)
    mixed = (scores * weights).astype(jnp.bfloat16)
    inside = jnp.einsum("hij,jhd->ihd", mixed, value_rows, preferred_element_type=jnp.float32)
    value_full = value_rows.astype(jnp.float32)
    reaches = jnp.exp(running) * (doc_rows == doc_id).astype(jnp.float32)[:, None]
    carried_part = jnp.einsum(
        "ihd,hde->ihe",
        query_rows.astype(jnp.float32) * reaches[:, :, None],
        kv_state,
        precision=highest,
    )
    final_doc = doc_rows[-1]
    retain = (doc_id == final_doc).astype(jnp.float32)
    fading = (
        jnp.exp(running[-1][None, :] - running)
        * (doc_rows == final_doc).astype(jnp.float32)[:, None]
    )
    fresh_part = jnp.einsum(
        "jhd,jhe->hde",
        key_rows.astype(jnp.float32) * fading[:, :, None],
        value_full,
        precision=highest,
    )
    new_state = retain * jnp.exp(running[-1])[:, None, None] * kv_state + fresh_part
    return ((new_state, final_doc), inside + carried_part)


def sweep(query3, key3, value3, rate_rows, doc_rows, start_state, start_doc):
    rows_here = doc_rows.shape[0]
    heads_here = query3.shape[1]
    block_len = min(512, rows_here)
    block_count = rows_here // block_len
    pieces = (
        query3.reshape(block_count, block_len, heads_here, DH),
        key3.reshape(block_count, block_len, heads_here, DH),
        value3.reshape(block_count, block_len, heads_here, DH),
        rate_rows.reshape(block_count, block_len, heads_here),
        doc_rows.reshape(block_count, block_len),
    )
    final_carry, attended = lax.scan(block_step, (start_state, start_doc), pieces)
    return (final_carry[0], attended.reshape(rows_here, heads_here, DH))


def combine_pair(earlier, later):
    rate_early, state_early, doc_early = earlier
    rate_late, state_late, doc_late = later
    linked = ((doc_early == doc_late) | (doc_early < 0) | (doc_late < 0)).astype(jnp.float32)
    merged = linked[0] * rate_late[:, None, None] * state_early + state_late
    return (rate_early * rate_late, merged, jnp.where(doc_late < 0, doc_early, doc_late))


def carry_in(shard_rates, shard_state, shard_doc):
    heads_here = shard_rates.shape[0]
    neutral = (
        jnp.ones((heads_here,), jnp.float32),
        jnp.zeros((heads_here, DH, DH), jnp.float32),
        jnp.full((1,), -1.0, jnp.float32),
    )
    prefix = entering((shard_rates, shard_state, shard_doc), "ctx", combine_pair, neutral)
    return (prefix[1], prefix[2])


def on_device(queries, keys, values, gates, log_decay, segment_ids, norm_gain, out_weight):
    rows_here = queries.shape[1]
    width = queries.shape[2]
    heads_here = width // DH
    query3 = queries[0].reshape(rows_here, heads_here, DH)
    key3 = keys[0].reshape(rows_here, heads_here, DH)
    value3 = values[0].reshape(rows_here, heads_here, DH)
    rate_rows = log_decay[0]
    doc_rows = segment_ids[0].astype(jnp.float32)
    running = jnp.cumsum(rate_rows, axis=0)
    shard_rates = jnp.exp(running[-1])
    shard_doc = doc_rows[-1:]
    fading = (
        jnp.exp(running[-1][None, :] - running)
        * (doc_rows == shard_doc[0]).astype(jnp.float32)[:, None]
    )
    shard_state = jnp.einsum(
        "jhd,jhe->hde",
        key3.astype(jnp.float32) * fading[:, :, None],
        value3.astype(jnp.float32),
        precision=highest,
    )
    incoming, incoming_doc = carry_in(shard_rates, shard_state, shard_doc)
    ignored, attended = sweep(query3, key3, value3, rate_rows, doc_rows, incoming, incoming_doc[0])
    scaling = lax.rsqrt(jnp.mean(attended * attended, axis=-1, keepdims=True) + 1e-06)
    normed = (
        (attended * scaling).reshape(rows_here, width)
        * norm_gain[0][None, :]
        * jax.nn.sigmoid(gates[0].astype(jnp.float32))
    ).astype(jnp.bfloat16)
    weight_here = out_weight[0]
    partial_value = jnp.dot(
        normed,
        lax.all_gather(weight_here, "ctx", axis=1, tiled=True),
        preferred_element_type=jnp.float32,
    )
    summed = lax.psum_scatter(
        partial_value.astype(jnp.bfloat16), "head", scatter_dimension=1, tiled=True
    )
    handed = from_behind(summed, "pipe", 1)
    return handed[None]


def solution(mesh):
    return jax.shard_map(
        on_device,
        mesh=mesh,
        in_specs=(
            P("pipe", "ctx", "head"),
            P("pipe", "ctx", "head"),
            P("pipe", "ctx", "head"),
            P("pipe", "ctx", "head"),
            P("pipe", "ctx", "head"),
            P("pipe", "ctx"),
            P("pipe", "head"),
            P("pipe", "head", "ctx"),
        ),
        out_specs=P("pipe", "ctx", "head"),
        check_vma=False,
    )
```

profile of v0, /device:TPU:33, one launch (start us, length us, event | category | flops | bytes accessed | tf_op | source)
XLA Modules:
  0.0 235.9 jit_solution(17835527506379368174)
XLA Ops:
  8.8 1.3 compare_convert_fusion.1
  10.2 1.1 copy.36
  11.3 1.0 copy.39
  12.3 1.1 convolution_convert_fusion
  15.0 1.3 dynamic-slice.1
  17.0 33.7 %all-reduce = bf16[16]{0:T(256)(128)(2,1)S(1)} all-reduce(bf16[16]{0:T(256)(128)(2,1)S(1)} %dynamic-update-slice), channel_id=1, replica_groups=mesh['ctx'=16,'head'=8,'pipe'=2] {'ctx'}, use_global_device_ids=true, to_apply=%add | all-reduce | flops 16 | bytes 64
  50.7 14.6 %all-gather.2 = bf16[16,1,8]{2,1,0:T(2,128)(2,1)S(1)} all-gather(bf16[1,1,8]{2,1,0:T(2,128)(2,1)S(1)} %get-tuple-element.212), channel_id=1, replica_groups=mesh['ctx'=16,'head'=8,'pipe'=2] {'ctx'}, dimensions={0}, use_global_device_ids=true | all-gather | bytes 272 | tf_op jit(solution)/shard_map/all_gather | solution.py:15
  65.3 1.0 copy.38
  66.5 6.6 %all-gather.6.cloned.1.call-done = bf16[128,128,128]{2,1,0:T(8,128)(2,1)} async-done(((bf16[8,128,128]{2,1,0:T(8,128)(2,1)}), bf16[128,128,128]{2,1,0:T(8,128)(2,1)}) %all-gather.6.cloned.1.call-update) | async-done | bytes 4194320 | tf_op jit(solution)/shard_map/all_gather | solution.py:15
  73.0 62.4 %while.10 = (s32[]{:T(128)}, f32[8,128,128]{2,1,0:T(8,128)S(1)}, f32[1]{0:T(128)}, s32[]{:T(128)}, bf16[16,1]{0,1:T(2,128)(2,1)S(1)}, /*index=5*/bf16[16,8]{1,0:...) while((s32[]{:T(128)}, f32[8,128,128]{2,1,0:T(8,128)S(1)}, ...), condition=%wide.region_2.3_spmd.clone, body=%wide.region_1.2_spmd.clone.sunk | while | flops 655388 | bytes 1310999 | solution.py:32
  75.1 1.1 fusion.44
  79.0 1.1 fusion.44
  82.9 1.1 fusion.44
  86.8 1.1 fusion.44
  90.7 1.1 fusion.44
  94.6 1.1 fusion.44
  98.5 1.1 fusion.44
  102.4 1.1 fusion.44
  106.4 1.1 fusion.44
  110.2 1.1 fusion.44
  114.1 1.1 fusion.44
  118.0 1.1 fusion.44
  121.9 1.1 fusion.44
  125.9 1.1 fusion.44
  129.8 1.1 fusion.44
  133.7 1.1 fusion.44
  135.6 1.3 convolution_bitcast_fusion.1
  137.7 41.3 %all-gather.8.cloned.1.call-done = bf16[1,1024,6144]{2,1,0:T(8,128)(2,1)} async-done(((bf16[1,1024,384]{2,1,0:T(8,128)(2,1)}), bf16[1,1024,6144]{2,1,0:T(8,128)(2,1)}) %all-gather.8.cloned.1.call-update) | async-done | bytes 12582928 | tf_op jit(solution)/shard_map/all_gather | solution.py:147
  179.0 7.6 %fusion.6 = bf16[128,6144]{1,0:T(8,128)(2,1)} fusion(bf16[1,1024,6144]{2,1,0:T(8,128)(2,1)} %all-gather.8.cloned.1.call-done, bf16[1,128,1024]{2,1,0:T(8,128)(2,1)S(1)} %copy-done, f32[128,1024]{1,0:T(8,128)S(1)} %copy.34, f32[1024]{0:T(1024)S(1)} %bitcast.81), kind=kOutput, calls=%fused_computation.9 | convolution fusion | flops 1612316672 | bytes 14946304 | tf_op jit(solution)/shard_map/dot_general | solution.py:145
  186.6 35.9 %reduce-scatter.2.cloned.1.call-done = bf16[128,768]{1,0:T(8,128)(2,1)} async-done(((bf16[128,6144]{1,0:T(8,128)(2,1)}), bf16[128,768]{1,0:T(8,128)(2,1)}) %reduce-scatter.2.cloned.1.call-update) | async-done | bytes 196624 | tf_op jit(solution)/shard_map/reduce_scatter | solution.py:150
  222.5 4.9 %collective-permute-start = (bf16[128,768]{1,0:T(8,128)(2,1)}, bf16[128,768]{1,0:T(8,128)(2,1)S(1)}, u32[]{:S(2)}, u32[]{:S(2)}) collective-permute-start(bf16[128,768]{1,0:T(8,128)(2,1)} %reduce-scatter.2.cloned.1.call-done), channel_id=1, source_target_pairs={{0,1},{1,0},{2,3},{3,2},{4,5},{5,4},{6,7},{7,6},{8,9},{9,8},{10,11... | collective-permute-start | bytes 589832 | tf_op jit(solution)/shard_map/ppermute | solution.py:37
  227.4 1.3 collective-permute-done
  (65 shorter events, 16.5 us)
Async XLA Ops:
  6.5 66.5 %all-gather.6.cloned.1.call-start = ((), (), s32[]{:S(2)}) async-start(), calls=%async_computation.2 | async-start | bytes 4456448 | tf_op jit(solution)/shard_map/all_gather | solution.py:15
  13.5 122.0 %copy-start.2 = (s32[1,128]{1,0:T(1,128)S(1)}, s32[1,128]{1,0:T(1,128)}, u32[]{:S(2)}) copy-start(s32[1,128]{1,0:T(1,128)} %param.15) | copy-start | bytes 1540
  13.5 165.5 %all-gather.8.cloned.1.call-start = ((), (), s32[]{:S(2)}) async-start(), calls=%async_computation.3 | async-start | bytes 13369344 | tf_op jit(solution)/shard_map/all_gather | solution.py:147
  14.2 208.3 %reduce-scatter.2.cloned.1.call-start = ((), (), s32[]{:S(2)}) async-start(), calls=%async_computation.1 | async-start | bytes 1769472 | tf_op jit(solution)/shard_map/reduce_scatter | solution.py:150
  135.5 43.5 %copy-start = (bf16[1,128,1024]{2,1,0:T(8,128)(2,1)S(1)}, bf16[1,128,1024]{2,1,0:T(8,128)(2,1)}, u32[]{:S(2)}) copy-start(bf16[1,128,1024]{2,1,0:T(8,128)(2,1)} %param.13) | copy-start | bytes 786436
  135.5 43.5 %copy-start.1 = (f32[1,1024]{1,0:T(1,128)S(1)}, f32[1,1024]{1,0:T(1,128)}, u32[]{:S(2)}) copy-start(f32[1,1024]{1,0:T(1,128)} %param.16) | copy-start | bytes 12292
  222.5 6.2 %collective-permute-start = (bf16[128,768]{1,0:T(8,128)(2,1)}, bf16[128,768]{1,0:T(8,128)(2,1)S(1)}, u32[]{:S(2)}, u32[]{:S(2)}) collective-permute-start(bf16[128,768]{1,0:T(8,128)(2,1)} %reduce-scatter.2.cloned.1.call-done), channel_id=1, source_target_pairs={{0,1},{1,0},{2,3},{3,2},{4,5},{5,4},{6,7},{7,6},{8,9},{9,8},{10,11... | collective-permute-start | bytes 589832 | tf_op jit(solution)/shard_map/ppermute | solution.py:37
Sparse Core Ops, SparseCore 0:
  13.6 59.3 all-gather.5
  75.4 103.4 all-gather.7
  186.7 35.7 reduce-scatter.1
where the time goes:
time: 239 us; the launch traced here: 236 us
  waiting for transfers between devices  85.7 us (36%)
  blocking collectives  48.3 us (20%)
  loops' own time  34.1 us (14%)
  other arithmetic  20.2 us (8%)
  local copies, waits for them, and re-layouts  18.2 us (8%)
  between operations  13.9 us (6%)
  matrix products  10.5 us (4%)
  starting transfers between devices  4.98 us (2%)
    all_gather x1, waiting for transfers between devices, on_device(): lax.all_gather(weight_here, 'ctx', axis=1, tiled=True)  41.3 us
    reduce_scatter x1, waiting for transfers between devices, on_device(): lax.psum_scatter(partial_value.astype(jnp.bfloat16), 'head', scatter_dime...  35.9 us
    another operation x1, loops' own time, entering(): return lax.fori_loop(0, count, hop, start)  34.1 us
    unnamed x1, blocking collectives  33.7 us
    select_n x16, other arithmetic, hop(): return jax.tree.map(lambda a, b: jnp.where(reached, a, b), new, before)  17.5 us
    all_gather x1, blocking collectives, entering(): lax.all_gather(part.astype(kind), axis)  14.6 us
    dynamic_slice x16, local copies, waits for them, and re-layouts, hop(): part[k].astype(own.dtype)  10.6 us
    dot_general x1, matrix products, on_device(): jnp.dot(normed, lax.all_gather(weight_here, 'ctx', axis=1, tiled=True), p...  7.64 us
  transfers between devices with their start and end apart: 4, of which 4 were waited for; matrix products, arithmetic and copies ran while one was open for 14% of the time, Pallas kernels for 0%

commit v1 on v0

v1 whole, which is shorter than its diff:
```python
import jax
import jax.numpy as jnp
from jax import lax
from jax.experimental import pallas as pl
from jax.experimental.pallas import tpu as pltpu
from jax.sharding import PartitionSpec as P

MESH = pl.DeviceIdType.MESH
F32 = jnp.float32
BF16 = jnp.bfloat16
HIGHEST = lax.Precision.HIGHEST

DH = 128
TOK = 128
ROW = 512
HW = 256
KD = 1024
NW = 384
SH = 64
DELTAS = (1, 3, 2)


def dot(a, b, dims=((1,), (0,)), precision=None):
    return lax.dot_general(
        a, b, (dims, ((), ())), precision=precision, preferred_element_type=F32
    )


def kernel(
    k_hbm, v_hbm, q_hbm, g_hbm, pk_ref, gain_ref, w_hbm, out_hbm,
    rx, pkx, kf, att, abuf, wbuf, st_out, st_in, pbuf, rl, rs, fin,
    lsem, wlsem, a2a_s, a2a_r, pk_s, pk_r, w_s, w_r, wr_s, wr_r, st_sem,
    ag_s, ag_r, agr_s, agr_r, rl_s, rl_r, rs_s, rs_r, fin_s, fin_r,
):
    c, z, p = lax.axis_index("ctx"), lax.axis_index("head"), lax.axis_index("pipe")
    x, y = lax.rem(c, 4), lax.div(c, 4)

    def at_x(d):
        return 4 * y + lax.rem(x + d, 4)

    def at_y(d):
        return 4 * lax.rem(y + d, 4) + x

    def at_z(d):
        return lax.rem(z + d + 8, 8)

    def remote(src, dst, send, recv, dev):
        return pltpu.make_async_remote_copy(
            src_ref=src, dst_ref=dst, send_sem=send, recv_sem=recv,
            device_id=dev, device_id_type=MESH,
        )

    def arrived(dst, recv):
        remote(dst, dst, recv, recv, (c, z, 1 - p)).wait_recv()

    sent = []

    def send(*a):
        copy = remote(*a)
        copy.start()
        sent.append(copy)

    local = []
    for a, ref in enumerate((k_hbm, v_hbm, q_hbm, g_hbm)):
        cp = pltpu.make_async_copy(
            ref.at[0, :, pl.ds(pl.multiple_of(x * HW, HW), HW)],
            rx.at[a, pl.ds(pl.multiple_of(x * TOK, TOK), TOK), :],
            lsem.at[a],
        )
        cp.start()
        local.append(cp)
    w_local = pltpu.make_async_copy(w_hbm.at[0], wbuf.at[0], wlsem)
    w_local.start()

    fin_ctx = 4 * y + lax.div(z, 2)

    def fin_head(yy):
        return 2 * yy + lax.div(x, 2)

    def phase_y(ph):
        return lax.rem(y + (0, 3, 1, 2)[ph], 4)

    barrier = pltpu.get_barrier_semaphore()
    peers = [(at_x(d), z, p) for d in DELTAS]
    peers += [(at_y(1), z, p), (at_y(3), z, p)]
    peers += [(c, at_z(1), p), (c, at_z(-1), p)]
    peers += [(fin_ctx, fin_head(yy), 1 - p) for yy in range(4)]
    for zz in range(2):
        for xx in range(2):
            peers.append(
                (4 * lax.div(z, 2) + 2 * lax.rem(z, 2) + xx, 2 * x + zz, 1 - p)
            )
    for dev in peers:
        pl.semaphore_signal(barrier, inc=1, device_id=dev, device_id_type=MESH)
    pl.semaphore_wait(barrier, len(peers))

    for i, d in enumerate(DELTAS):
        to = lax.rem(x + d, 4)
        send(pk_ref.at[to], pkx.at[x], pk_s.at[i], pk_r.at[i], (at_x(d), z, p))

    def a2a(a, ref):
        for i, d in enumerate(DELTAS):
            to = lax.rem(x + d, 4)
            send(
                ref.at[0, :, pl.ds(pl.multiple_of(to * HW, HW), HW)],
                rx.at[a, pl.ds(pl.multiple_of(x * TOK, TOK), TOK), :],
                a2a_s.at[a, i], a2a_r.at[a, i], (at_x(d), z, p),
            )

    def a2a_wait(a):
        for i, d in enumerate(DELTAS):
            src = lax.rem(x + 4 - d, 4)
            arrived(
                rx.at[a, pl.ds(pl.multiple_of(src * TOK, TOK), TOK), :], a2a_r.at[a, i]
            )

    a2a(0, k_hbm)
    a2a(1, v_hbm)
    for i in range(4):
        for side, (d, ch) in enumerate(((1, i), (3, (i + 2) % 4))):
            rows = pl.ds(ch * HW, HW)
            send(
                w_hbm.at[0, rows, :], wbuf.at[1 + side, rows, :],
                w_s.at[side, ch], w_r.at[side, ch], (at_y(d), z, p),
            )
    a2a(2, q_hbm)
    a2a(3, g_hbm)

    def w_wait(side, ch):
        arrived(wbuf.at[1 + side, pl.ds(ch * HW, HW), :], w_r.at[side, ch])

    def w_relay(side, ch):
        rows = pl.ds(ch * HW, HW)
        send(
            wbuf.at[1 + side, rows, :], wbuf.at[3, rows, :],
            wr_s.at[ch], wr_r.at[ch], (at_y((1, 3)[side]), z, p),
        )

    for i, d in enumerate(DELTAS):
        arrived(pkx.at[lax.rem(x + 4 - d, 4)], pk_r.at[i])
    pkx[x] = pk_ref[x]
    ia = lax.broadcasted_iota(jnp.int32, (TOK, TOK), 0)
    ib = lax.broadcasted_iota(jnp.int32, (TOK, TOK), 1)
    upper = (ia <= ib).astype(F32)
    lower = (ia >= ib).astype(F32)
    eye = (ia == ib).astype(F32)
    rows_, cols_, segr, segc = [], [], [], []
    off_r, off_c = jnp.zeros((8, 1), F32), jnp.zeros((1, 8), F32)
    for b in range(4):
        part = pkx[b]
        r = dot(part, upper, precision=HIGHEST) + off_r
        s = dot(lower, part, ((1,), (1,)), precision=HIGHEST) + off_c
        e = dot(eye, part, ((1,), (1,)), precision=HIGHEST)
        off_r, off_c = r[:, TOK - 1 : TOK], s[TOK - 1 : TOK, :]
        rows_.append(r)
        cols_.append(s)
        segr.append(part[2:3, :])
        segc.append(e[:, 2:3])
    last_doc = segr[3][:, TOK - 1 : TOK]

    local[0].wait()
    local[1].wait()
    a2a_wait(0)
    a2a_wait(1)
    for b in range(4):
        keep = (segc[b] == last_doc).astype(F32)
        rr = pl.ds(b * TOK, TOK)
        for h in range(2):
            fade = jnp.exp(jnp.minimum(off_c[:, h : h + 1] - cols_[b][:, h : h + 1], 0.0)) * keep
            hh = slice(h * DH, (h + 1) * DH)
            kf[rr, hh] = (rx[0, rr, hh].astype(F32) * fade).astype(BF16)
    for h in range(2):
        hh = slice(h * DH, (h + 1) * DH)
        st_out[hh, :] = dot(kf[:, hh], rx[1, :, hh], ((0,), (0,))).astype(BF16)
    st_out[256:272, :] = jnp.broadcast_to(last_doc, (16, DH)).astype(BF16)
    send(st_out, st_in, st_sem.at[0], st_sem.at[1], (at_y(1), z, p))

    local[2].wait()
    a2a_wait(2)
    for i in range(4):
        n = (i + 1) * TOK
        rr = pl.ds(i * TOK, TOK)
        seg_row = jnp.concatenate(segr[: i + 1], axis=1)
        it = lax.broadcasted_iota(jnp.int32, (TOK, n), 0) + i * TOK
        ij = lax.broadcasted_iota(jnp.int32, (TOK, n), 1)
        allowed = (ij <= it) & (segc[i] == seg_row)
        for h in range(2):
            hh = slice(h * DH, (h + 1) * DH)
            crow = jnp.concatenate([r[h : h + 1, :] for r in rows_[: i + 1]], axis=1)
            gap = jnp.minimum(cols_[i][:, h : h + 1] - crow, 0.0)
            weight = jnp.where(allowed, jnp.exp(gap), 0.0)
            scores = dot(rx[2, rr, hh], rx[0, 0:n, hh], ((1,), (1,)))
            mixed = (scores * weight).astype(BF16)
            att[rr, hh] = dot(mixed, rx[1, 0:n, hh])

    for side in range(2):
        for ch in (0, 1) if side == 0 else (2, 3):
            w_wait(side, ch)
            w_relay(side, ch)

    local[3].wait()
    a2a_wait(3)
    arrived(st_in, st_sem.at[1])
    prev_doc = st_in[256:257, 0:1].astype(F32)
    later = (y > 0).astype(F32)
    for i in range(4):
        rr = pl.ds(i * TOK, TOK)
        same = (segc[i] == prev_doc).astype(F32) * later
        for h in range(2):
            hh = slice(h * DH, (h + 1) * DH)
            reach = jnp.exp(cols_[i][:, h : h + 1]) * same
            full = att[rr, hh] + dot(rx[2, rr, hh], st_in[hh, :]) * reach
            scale = lax.rsqrt(jnp.mean(full * full, axis=-1, keepdims=True) + 1e-06)
            gain = gain_ref[:, pl.ds(pl.multiple_of(x * HW + h * DH, DH), DH)]
            gate = 1.0 / (1.0 + jnp.exp(-rx[3, rr, hh].astype(F32)))
            abuf[0, rr, hh] = (full * scale * gain * gate).astype(BF16)
        for side, d in enumerate((1, 3)):
            send(
                abuf.at[0, rr, :], abuf.at[1 + side, rr, :],
                ag_s.at[side, i], ag_r.at[side, i], (at_x(d), z, p),
            )
    for side in range(2):
        for ch in (0, 1) if side == 0 else (2, 3):
            rr = pl.ds(ch * TOK, TOK)
            arrived(abuf.at[1 + side, rr, :], ag_r.at[side, ch])
            send(
                abuf.at[1 + side, rr, :], abuf.at[3, rr, :],
                agr_s.at[ch], agr_r.at[ch], (at_x((1, 3)[side]), z, p),
            )
    for side in range(2):
        for ch in (2, 3) if side == 0 else (0, 1):
            arrived(abuf.at[1 + side, pl.ds(ch * TOK, TOK), :], ag_r.at[side, ch])
    for ch in range(4):
        arrived(abuf.at[3, pl.ds(ch * TOK, TOK), :], agr_r.at[ch])

    xs = [lax.rem(x + d, 4) for d in (0, 3, 1, 2)]

    def project(ph):
        def body(i, carry):
            rr = pl.ds(pl.multiple_of(i * TOK, TOK), TOK)
            acc = jnp.zeros((TOK, NW), F32)
            for s in range(4):
                kk = pl.ds(pl.multiple_of(xs[s] * HW, HW), HW)
                acc = acc + dot(abuf[s, rr, :], wbuf[ph, kk, :])
            pbuf[ph, rr, :] = acc.astype(BF16)
            return carry

        lax.fori_loop(0, 4, body, 0)

    def share(owner):
        return pl.ds(pl.multiple_of(lax.rem(owner + 16, 8) * SH, SH), SH)

    def long_send(ph, t):
        s = (1, -1)[ph % 2]
        src = pbuf.at[ph, share(z - s * 4), :] if t == 0 else rl.at[ph, t - 1]
        send(src, rl.at[ph, t], rl_s.at[ph, t], rl_r.at[ph, t], (c, at_z(-s), p))

    def short_send(ph, t):
        s = (1, -1)[ph % 2]
        src = pbuf.at[ph, share(z + s * 3), :] if t == 0 else rs.at[ph, t - 1]
        send(src, rs.at[ph, t], rs_s.at[ph, t], rs_r.at[ph, t], (c, at_z(s), p))

    def step(ph, t):
        s = (1, -1)[ph % 2]
        arrived(rl.at[ph, t], rl_r.at[ph, t])
        if t < 3:
            rl[ph, t] = (
                rl[ph, t].astype(F32) + pbuf[ph, share(z - s * (3 - t)), :].astype(F32)
            ).astype(BF16)
            long_send(ph, t + 1)
        if t < 2:
            arrived(rs.at[ph, t], rs_r.at[ph, t])
            rs[ph, t] = (
                rs[ph, t].astype(F32) + pbuf[ph, share(z + s * (2 - t)), :].astype(F32)
            ).astype(BF16)
            short_send(ph, t + 1)
        if t == 3:
            arrived(rs.at[ph, 2], rs_r.at[ph, 2])
            fin[ph] = (
                rl[ph, 3].astype(F32) + rs[ph, 2].astype(F32) + pbuf[ph, share(z), :].astype(F32)
            ).astype(BF16)
            send(
                fin.at[ph],
                out_hbm.at[
                    0,
                    pl.ds(pl.multiple_of(lax.rem(z, 2) * SH, SH), SH),
                    pl.ds(pl.multiple_of(lax.rem(x, 2) * NW, NW), NW),
                ],
                fin_s.at[ph], fin_r.at[lax.rem(z, 2), lax.rem(x, 2)],
                (fin_ctx, fin_head(phase_y(ph)), 1 - p),
            )

    w_local.wait()
    project(0)
    long_send(0, 0)
    short_send(0, 0)
    for side in range(2):
        for ch in (2, 3) if side == 0 else (0, 1):
            w_wait(side, ch)
        project(1 + side)
        long_send(1 + side, 0)
        short_send(1 + side, 0)
    for t in range(4):
        for ph in range(3):
            step(ph, t)
    for ch in range(4):
        arrived(wbuf.at[3, pl.ds(ch * HW, HW), :], wr_r.at[ch])
    project(3)
    long_send(3, 0)
    short_send(3, 0)
    for t in range(4):
        step(3, t)

    for zz in range(2):
        for xx in range(2):
            arrived(
                out_hbm.at[0, pl.ds(zz * SH, SH), pl.ds(xx * NW, NW)], fin_r.at[zz, xx]
            )
    for copy in sent:
        copy.wait_send()


def on_device(queries, keys, values, gates, log_decay, segment_ids, norm_gain, out_weight):
    decay = log_decay[0].T.reshape(4, 2, TOK)
    docs = jnp.broadcast_to(segment_ids.astype(F32)[None], (4, 1, TOK))
    packed = jnp.concatenate([decay, docs, jnp.zeros((4, 5, TOK), F32)], axis=1)
    hbm = pl.BlockSpec(memory_space=pltpu.HBM)
    vmem = pl.BlockSpec(memory_space=pltpu.VMEM)
    dma = pltpu.SemaphoreType.DMA
    return pl.pallas_call(
        kernel,
        out_shape=jax.ShapeDtypeStruct((1, TOK, 2 * NW), BF16),
        in_specs=[hbm, hbm, hbm, hbm, vmem, vmem, hbm],
        out_specs=hbm,
        scratch_shapes=[
            pltpu.VMEM((4, ROW, HW), BF16),
            pltpu.VMEM((4, 8, TOK), F32),
            pltpu.VMEM((ROW, HW), BF16),
            pltpu.VMEM((ROW, HW), F32),
            pltpu.VMEM((4, ROW, HW), BF16),
            pltpu.VMEM((4, KD, NW), BF16),
            pltpu.VMEM((272, DH), BF16),
            pltpu.VMEM((272, DH), BF16),
            pltpu.VMEM((4, ROW, NW), BF16),
            pltpu.VMEM((4, 4, SH, NW), BF16),
            pltpu.VMEM((4, 3, SH, NW), BF16),
            pltpu.VMEM((4, SH, NW), BF16),
            dma((4,)), dma,
            dma((4, 3)), dma((4, 3)), dma((3,)), dma((3,)),
            dma((2, 4)), dma((2, 4)), dma((4,)), dma((4,)), dma((2,)),
            dma((2, 4)), dma((2, 4)), dma((4,)), dma((4,)),
            dma((4, 4)), dma((4, 4)), dma((4, 3)), dma((4, 3)),
            dma((4,)), dma((2, 2)),
        ],
        compiler_params=pltpu.CompilerParams(
            collective_id=0, has_side_effects=True, vmem_limit_bytes=60 * 2**20
        ),
        cost_estimate=pl.CostEstimate(
            flops=2 * 10**9, bytes_accessed=3 * 2**20, transcendentals=10**6
        ),
    )(keys, values, queries, gates, packed, norm_gain, out_weight)


def solution(mesh):
    return jax.shard_map(
        on_device,
        mesh=mesh,
        in_specs=(
            P("pipe", "ctx", "head"),
            P("pipe", "ctx", "head"),
            P("pipe", "ctx", "head"),
            P("pipe", "ctx", "head"),
            P("pipe", "ctx", "head"),
            P("pipe", "ctx"),
            P("pipe", "head"),
            P("pipe", "head", "ctx"),
        ),
        out_specs=P("pipe", "ctx", "head"),
        check_vma=False,
    )
```

time: 239 us -> 86.1 us (0.36)
  the two profiles are of different devices: /device:TPU:33 before, /device:TPU:17 now
where the time goes in v1:
time: 86.1 us; the launch traced here: 85.8 us
  Pallas kernels  82.2 us (95%)
  local copies, waits for them, and re-layouts  2.95 us (3%)
    pallas_call x1, Pallas kernels, on_device(): pl.pallas_call(kernel, out_shape=jax.ShapeDtypeStruct((1, TOK, 2 * NW), B...  82.2 us
    unnamed x5, local copies, waits for them, and re-layouts  2.87 us

profile of v1, /device:TPU:17, one launch (start us, length us, event | category | flops | bytes accessed | tf_op | source)
XLA Modules:
  0.0 85.8 jit_solution(18203448359434278806)
XLA Ops:
  0.0 0.0 copy-start.1
  0.0 0.7 copy-done.1
  0.7 0.0 copy-start
  0.7 0.1 pad.2.clone
  0.7 0.6 copy-done
  1.3 0.7 maximum_maximum_fusion.pk_ref
  2.0 82.2 %shard_map.82 = bf16[1,128,768]{2,1,0:T(8,128)(2,1)} custom-call(bf16[1,128,1024]{2,1,0:T(8,128)(2,1)} %k_hbm.1, bf16[1,128,1024]{2,1,0:T(8,128)(2,1)} %v_hbm.1, bf16[1,128,1024]{2,1,0:T(8,128)(2,1)} %q_hbm.1, bf16[1,128,1024]{2,1,0:T(8,128)(2,1)} %g_hbm.1, f32[4,8,128]{2,1,0:T(8,128)} %maximum_maximum_fusion.pk_ref, f32[1,1024]{1,0:T(1,128)} %gain_ref.1, ...), custom_call_target="tpu_custom_call" | custom-call | flops 2000000000 | bytes 3145728 | tf_op jit(solution)/shard_map/pallas_call | solution.py:330
  84.2 1.6 %copy.10 = bf16[1,128,768]{2,1,0:T(8,128)(2,1)} copy(bf16[1,128,768]{2,1,0:T(8,128)(2,1)} %shard_map.82) | data formatting | bytes 393216
  (3 shorter events, 0.0 us)
Async XLA Ops:
  0.0 0.7 copy-start.1
  0.7 0.7 copy-start

commit v2 on v1

v2 whole, which is shorter than its diff:
```python
import jax
import jax.numpy as jnp
from jax import lax
from jax.experimental import pallas as pl
from jax.experimental.pallas import tpu as pltpu
from jax.sharding import PartitionSpec as P

MESH = pl.DeviceIdType.MESH
F32 = jnp.float32
BF16 = jnp.bfloat16
HIGHEST = lax.Precision.HIGHEST

DH = 128
TOK = 128
HW = 256
KD = 1024
NW = 384
N3 = 3 * NW
CH = 32
SH = 16
DELTAS = (1, 3, 2)


def dot(a, b, dims=((1,), (0,)), precision=None):
    return lax.dot_general(
        a, b, (dims, ((), ())), precision=precision, preferred_element_type=F32
    )


def kernel(
    k_hbm, v_hbm, q_hbm, g_hbm, decay_hbm, docs_hbm, gain_hbm, w_hbm, out_hbm,
    rx, pk, docs, gain, pkx, kf, att, abuf, wbuf, st_out, st_in,
    pa, la, sa, fa, pb, lb, sb, fb,
    lsem, a2a_s, a2a_r, pk_s, pk_r, w_s, w_r, wr_s, wr_r, st_sem,
    ag_s, ag_r, l_s, l_r, s_s, s_r, fin_s, fin_r,
):
    c, z, p = lax.axis_index("ctx"), lax.axis_index("head"), lax.axis_index("pipe")
    x, y = lax.rem(c, 4), lax.div(c, 4)

    def at_x(d):
        return 4 * y + lax.rem(x + d, 4)

    def at_y(d):
        return 4 * lax.rem(y + d, 4) + x

    def at_z(d):
        return lax.rem(z + d + 8, 8)

    def block(i, size):
        return pl.ds(pl.multiple_of(i * size, size), size)

    def remote(src, dst, send, recv, dev):
        return pltpu.make_async_remote_copy(
            src_ref=src, dst_ref=dst, send_sem=send, recv_sem=recv,
            device_id=dev, device_id_type=MESH,
        )

    def arrived(dst, recv):
        remote(dst, dst, recv, recv, (c, z, 1 - p)).wait_recv()

    sent = []

    def send(*a):
        copy = remote(*a)
        copy.start()
        sent.append(copy)

    local = [
        pltpu.make_async_copy(src, dst, lsem.at[i])
        for i, (src, dst) in enumerate(
            [
                (ref.at[0, :, block(x, HW)], rx.at[a, x])
                for a, ref in enumerate((k_hbm, v_hbm, q_hbm, g_hbm))
            ]
            + [
                (decay_hbm, pk.at[0:8, :]),
                (docs_hbm, docs),
                (gain_hbm.at[:, block(x, HW)], gain),
                (w_hbm.at[0], wbuf.at[0]),
            ]
        )
    ]
    for i in (4, 5, 6, 0, 1, 2, 3, 7):
        local[i].start()

    def fin_dev(yy):
        return (4 * y + lax.div(z, 2), 2 * yy + lax.div(x, 2), 1 - p)

    def phase_y(ph):
        return lax.rem(y + (0, 3, 1, 2)[ph], 4)

    barrier = pltpu.get_barrier_semaphore()
    peers = [(at_x(d), z, p) for d in DELTAS]
    peers += [(at_y(1), z, p), (at_y(3), z, p)]
    peers += [(c, at_z(1), p), (c, at_z(-1), p)]
    peers += [fin_dev(yy) for yy in range(4)]
    for zz in range(2):
        for xx in range(2):
            peers.append(
                (4 * y + 2 * lax.rem(z, 2) + xx, 2 * x + zz, 1 - p)
            )
    for dev in peers:
        pl.semaphore_signal(barrier, inc=1, device_id=dev, device_id_type=MESH)
    local[4].wait()
    local[5].wait()
    pk[8:16, :] = jnp.broadcast_to(docs[...].astype(F32), (8, TOK))
    pl.semaphore_wait(barrier, len(peers))

    for i, d in enumerate(DELTAS):
        send(pk, pkx.at[x], pk_s.at[i], pk_r.at[i], (at_x(d), z, p))

    def a2a(a, ref):
        for i, d in enumerate(DELTAS):
            to = lax.rem(x + d, 4)
            send(
                ref.at[0, :, block(to, HW)], rx.at[a, x],
                a2a_s.at[a, i], a2a_r.at[a, i], (at_x(d), z, p),
            )

    def a2a_wait(a):
        local[a].wait()
        for i, d in enumerate(DELTAS):
            arrived(rx.at[a, lax.rem(x + 4 - d, 4)], a2a_r.at[a, i])

    def w_send(side, ch):
        rows = pl.ds(ch * HW, HW)
        send(
            w_hbm.at[0, rows, :], wbuf.at[1 + side, rows, :],
            w_s.at[side, ch], w_r.at[side, ch], (at_y((1, 3)[side]), z, p),
        )

    def w_wait(side, ch):
        arrived(wbuf.at[1 + side, pl.ds(ch * HW, HW), :], w_r.at[side, ch])

    def w_relay(side, ch):
        rows = pl.ds(ch * HW, HW)
        w_wait(side, ch)
        send(
            wbuf.at[1 + side, rows, :], wbuf.at[3, rows, :],
            wr_s.at[ch], wr_r.at[ch], (at_y((1, 3)[side]), z, p),
        )

    a2a(0, k_hbm)
    a2a(1, v_hbm)
    w_send(0, 0)
    w_send(1, 2)
    a2a(2, q_hbm)
    a2a(3, g_hbm)
    w_send(0, 1)
    w_send(1, 3)
    w_send(1, 0)
    w_send(1, 1)

    i8 = lax.broadcasted_iota(jnp.int32, (8, 8), 0)
    j8 = lax.broadcasted_iota(jnp.int32, (8, 8), 1)
    pick = (j8 == 2 * x + i8).astype(F32)
    ia = lax.broadcasted_iota(jnp.int32, (TOK, TOK), 0)
    ib = lax.broadcasted_iota(jnp.int32, (TOK, TOK), 1)
    upper = (ia <= ib).astype(F32)
    lower = (ia >= ib).astype(F32)
    eye = (ia == ib).astype(F32)
    for i, d in enumerate(DELTAS):
        arrived(pkx.at[lax.rem(x + 4 - d, 4)], pk_r.at[i])
    pkx[x] = pk[...]
    rows_, cols_, segr, segc = [], [], [], []
    off_r, off_c = jnp.zeros((8, 1), F32), jnp.zeros((1, 8), F32)
    for b in range(4):
        part = dot(pick, pkx[b, 0:8, :], precision=HIGHEST)
        r = dot(part, upper, precision=HIGHEST) + off_r
        s = dot(lower, part, ((1,), (1,)), precision=HIGHEST) + off_c
        e = dot(eye, pkx[b, 8:16, :], ((1,), (1,)), precision=HIGHEST)
        off_r, off_c = r[:, TOK - 1 : TOK], s[TOK - 1 : TOK, :]
        rows_.append(r)
        cols_.append(s)
        segr.append(pkx[b, 8:9, :])
        segc.append(e[:, 0:1])
    last_doc = segr[3][:, TOK - 1 : TOK]

    a2a_wait(0)
    a2a_wait(1)
    for b in range(4):
        keep = (segc[b] == last_doc).astype(F32)
        for h in range(2):
            hs = slice(h, h + 1)
            hh = slice(h * DH, (h + 1) * DH)
            fade = jnp.exp(jnp.minimum(off_c[:, hs] - cols_[b][:, hs], 0.0)) * keep
            kf[b * TOK : (b + 1) * TOK, hh] = (rx[0, b, :, hh].astype(F32) * fade).astype(BF16)
    for h in range(2):
        hh = slice(h * DH, (h + 1) * DH)
        values = rx[1, :, :, hh].reshape(4 * TOK, DH)
        st_out[hh, :] = dot(kf[:, hh], values, ((0,), (0,))).astype(BF16)
    st_out[256:272, :] = jnp.broadcast_to(last_doc, (16, DH)).astype(BF16)
    send(st_out, st_in, st_sem.at[0], st_sem.at[1], (at_y(1), z, p))
    w_send(0, 2)
    w_send(0, 3)

    a2a_wait(2)
    for i in range(4):
        n = (i + 1) * TOK
        seg_row = jnp.concatenate(segr[: i + 1], axis=1)
        it = lax.broadcasted_iota(jnp.int32, (TOK, n), 0) + i * TOK
        ij = lax.broadcasted_iota(jnp.int32, (TOK, n), 1)
        allowed = (ij <= it) & (segc[i] == seg_row)
        for h in range(2):
            hh = slice(h * DH, (h + 1) * DH)
            crow = jnp.concatenate([r[h : h + 1, :] for r in rows_[: i + 1]], axis=1)
            gap = jnp.minimum(cols_[i][:, h : h + 1] - crow, 0.0)
            weight = jnp.where(allowed, jnp.exp(gap), 0.0)
            key_rows = rx[0, 0 : i + 1, :, hh].reshape(n, DH)
            scores = dot(rx[2, i, :, hh], key_rows, ((1,), (1,)))
            mixed = (scores * weight).astype(BF16)
            att[i, :, hh] = dot(mixed, rx[1, 0 : i + 1, :, hh].reshape(n, DH))

    a2a_wait(3)
    arrived(st_in, st_sem.at[1])
    local[6].wait()
    prev_doc = st_in[256:257, 0:1].astype(F32)
    later = (y > 0).astype(F32)
    for i in range(4):
        same = (segc[i] == prev_doc).astype(F32) * later
        for h in range(2):
            hh = slice(h * DH, (h + 1) * DH)
            reach = jnp.exp(cols_[i][:, h : h + 1]) * same
            full = att[i, :, hh] + dot(rx[2, i, :, hh], st_in[hh, :]) * reach
            scale = lax.rsqrt(jnp.mean(full * full, axis=-1, keepdims=True) + 1e-06)
            gate = 1.0 / (1.0 + jnp.exp(-rx[3, i, :, hh].astype(F32)))
            abuf[0, i, :, hh] = (full * scale * gain[:, hh] * gate).astype(BF16)

    for j in range(4):
        for i, d in enumerate(DELTAS):
            rr = pl.ds(j * CH, CH)
            send(
                abuf.at[0, :, rr, :], abuf.at[1 + i, :, rr, :],
                ag_s.at[i, j], ag_r.at[i, j], (at_x(d), z, p),
            )

    for ch in range(2):
        w_relay(0, ch)
        w_relay(1, 2 + ch)

    xs = [lax.rem(x + d, 4) for d in (0, 3, 1, 2)]
    local[7].wait()

    def project_a(j):
        for i in range(3):
            arrived(abuf.at[1 + i, :, pl.ds(j * CH, CH), :], ag_r.at[i, j])
        if j == 0:
            for ch in range(2):
                w_wait(0, 2 + ch)
                w_wait(1, ch)

        def body(ph, carry):
            acc = jnp.zeros((4 * CH, NW), F32)
            for s in range(4):
                lhs = abuf[s, :, j * CH : (j + 1) * CH, :].reshape(4 * CH, HW)
                acc = acc + dot(lhs, wbuf[ph, block(xs[s], HW), :])
            pa[j, :, block(ph, NW)] = acc.astype(BF16)
            return carry

        lax.fori_loop(0, 3, body, 0)

    def project_b():
        for ch in range(4):
            arrived(wbuf.at[3, pl.ds(ch * HW, HW), :], wr_r.at[ch])

        def body(b, carry):
            acc = jnp.zeros((TOK, NW), F32)
            for s in range(4):
                acc = acc + dot(abuf[s, b], wbuf[3, block(xs[s], HW), :])
            acc = acc.astype(BF16)
            for half in range(2):
                for j in range(4):
                    low = j * CH + half * SH
                    pb[2 * b + half, j] = acc[low : low + SH, :]
            return carry

        lax.fori_loop(0, 4, body, 0)

    def own(b, owner):
        o = lax.rem(owner + 16, 8)
        return pb.at[o] if b == 4 else pa.at[b, block(o, SH), :]

    def longs(b, t):
        return lb.at[t] if b == 4 else la.at[b, t]

    def shorts(b, t):
        return sb.at[t] if b == 4 else sa.at[b, t]

    def sign(b):
        return (1, -1)[b % 2]

    def long_send(b, t):
        s = sign(b)
        src = own(b, z - s * 4) if t == 0 else longs(b, t - 1)
        send(src, longs(b, t), l_s.at[b, t], l_r.at[b, t], (c, at_z(-s), p))

    def short_send(b, t):
        s = sign(b)
        src = own(b, z + s * 3) if t == 0 else shorts(b, t - 1)
        send(src, shorts(b, t), s_s.at[b, t], s_r.at[b, t], (c, at_z(s), p))

    def start(b):
        if b == 4:
            project_b()
        else:
            project_a(b)
        long_send(b, 0)
        short_send(b, 0)

    def step(b, t):
        s = sign(b)
        arrived(longs(b, t), l_r.at[b, t])
        if t < 3:
            ref = longs(b, t)
            mine = own(b, z - s * (3 - t))
            ref[...] = (ref[...].astype(F32) + mine[...].astype(F32)).astype(BF16)
            long_send(b, t + 1)
        if t < 2:
            arrived(shorts(b, t), s_r.at[b, t])
            ref = shorts(b, t)
            mine = own(b, z + s * (2 - t))
            ref[...] = (ref[...].astype(F32) + mine[...].astype(F32)).astype(BF16)
            short_send(b, t + 1)
        if t == 3:
            arrived(shorts(b, 2), s_r.at[b, 2])
            total = longs(b, 3)[...].astype(F32) + shorts(b, 2)[...].astype(F32)
            total = (total + own(b, z)[...].astype(F32)).astype(BF16)
            if b == 4:
                fb[...] = total
            else:
                fa[b] = total
            for n in range(4 if b == 4 else 3):
                j, ph = (n, 3) if b == 4 else (b, n)
                src = fb.at[j] if b == 4 else fa.at[b, :, pl.ds(ph * NW, NW)]
                low = pl.multiple_of(j * CH + lax.rem(z, 2) * SH, SH)
                send(
                    src, out_hbm.at[0, pl.ds(low, SH), block(lax.rem(x, 2), NW)],
                    fin_s.at[j, ph], fin_r.at[j, lax.rem(z, 2), lax.rem(x, 2)],
                    fin_dev(phase_y(ph)),
                )

    for slot in range(9):
        for b in range(5):
            if 0 <= slot - 1 - b < 4:
                step(b, slot - 1 - b)
        if slot < 5:
            start(slot)

    for j in range(4):
        for zz in range(2):
            for xx in range(2):
                arrived(
                    out_hbm.at[0, pl.ds(j * CH + zz * SH, SH), pl.ds(xx * NW, NW)],
                    fin_r.at[j, zz, xx],
                )
    for copy in sent:
        copy.wait_send()


def on_device(queries, keys, values, gates, log_decay, segment_ids, norm_gain, out_weight):
    hbm = pl.BlockSpec(memory_space=pltpu.HBM)
    vmem = pltpu.VMEM
    dma = pltpu.SemaphoreType.DMA
    return pl.pallas_call(
        kernel,
        out_shape=jax.ShapeDtypeStruct((1, TOK, 2 * NW), BF16),
        in_specs=[hbm] * 8,
        out_specs=hbm,
        scratch_shapes=[
            vmem((4, 4, TOK, HW), BF16),
            vmem((16, TOK), F32),
            vmem((1, TOK), jnp.int32),
            vmem((1, HW), F32),
            vmem((4, 16, TOK), F32),
            vmem((4 * TOK, HW), BF16),
            vmem((4, TOK, HW), F32),
            vmem((4, 4, TOK, HW), BF16),
            vmem((4, KD, NW), BF16),
            vmem((272, DH), BF16),
            vmem((272, DH), BF16),
            vmem((4, TOK, N3), BF16),
            vmem((4, 4, SH, N3), BF16),
            vmem((4, 3, SH, N3), BF16),
            vmem((4, SH, N3), BF16),
            vmem((8, 4, SH, NW), BF16),
            vmem((4, 4, SH, NW), BF16),
            vmem((3, 4, SH, NW), BF16),
            vmem((4, SH, NW), BF16),
            dma((8,)), dma((4, 3)), dma((4, 3)), dma((3,)), dma((3,)),
            dma((2, 4)), dma((2, 4)), dma((4,)), dma((4,)), dma((2,)),
            dma((3, 4)), dma((3, 4)),
            dma((5, 4)), dma((5, 4)), dma((5, 3)), dma((5, 3)),
            dma((4, 4)), dma((4, 2, 2)),
        ],
        compiler_params=pltpu.CompilerParams(
            collective_id=0, has_side_effects=True, vmem_limit_bytes=60 * 2**20
        ),
        cost_estimate=pl.CostEstimate(
            flops=2 * 10**9, bytes_accessed=3 * 2**20, transcendentals=10**6
        ),
    )(
        keys, values, queries, gates, log_decay[0].T, segment_ids, norm_gain, out_weight
    )


def solution(mesh):
    return jax.shard_map(
        on_device,
        mesh=mesh,
        in_specs=(
            P("pipe", "ctx", "head"),
            P("pipe", "ctx", "head"),
            P("pipe", "ctx", "head"),
            P("pipe", "ctx", "head"),
            P("pipe", "ctx", "head"),
            P("pipe", "ctx"),
            P("pipe", "head"),
            P("pipe", "head", "ctx"),
        ),
        out_specs=P("pipe", "ctx", "head"),
        check_vma=False,
    )
```

time: 86.1 us -> 72.8 us (0.85)
  the two profiles are of different devices: /device:TPU:17 before, /device:TPU:23 now
where the time goes in v2:
time: 72.8 us; the launch traced here: 72.7 us
  Pallas kernels  71.1 us (98%)
  local copies, waits for them, and re-layouts  1.62 us (2%)
    pallas_call x1, Pallas kernels, on_device(): pl.pallas_call(kernel, out_shape=jax.ShapeDtypeStruct((1, TOK, 2 * NW), B...  71.1 us
    unnamed x1, local copies, waits for them, and re-layouts  1.62 us

profile of v2, /device:TPU:23, one launch (start us, length us, event | category | flops | bytes accessed | tf_op | source)
XLA Modules:
  0.0 72.7 jit_solution(12416945292289470802)
XLA Ops:
  0.0 71.1 %shard_map.82 = bf16[1,128,768]{2,1,0:T(8,128)(2,1)} custom-call(bf16[1,128,1024]{2,1,0:T(8,128)(2,1)} %k_hbm.1, bf16[1,128,1024]{2,1,0:T(8,128)(2,1)} %v_hbm.1, bf16[1,128,1024]{2,1,0:T(8,128)(2,1)} %q_hbm.1, bf16[1,128,1024]{2,1,0:T(8,128)(2,1)} %g_hbm.1, f32[8,128]{1,0:T(8,128)} %bitcast.3, s32[1,128]{1,0:T(1,128)} %docs_hbm.1, f32[1,1024]{1,0:T(1,128)} %gain_hbm.1, ...), custom_call_target="tpu_custom_call" | custom-call | flops 2000000000 | bytes 3145728 | tf_op jit(solution)/shard_map/pallas_call | solution.py:364
  71.1 1.6 %copy.10 = bf16[1,128,768]{2,1,0:T(8,128)(2,1)} copy(bf16[1,128,768]{2,1,0:T(8,128)(2,1)} %shard_map.82) | data formatting | bytes 393216

commit v3 on v2

v3 whole, which is shorter than its diff:
```python
import jax
import jax.numpy as jnp
from jax import lax
from jax.experimental import pallas as pl
from jax.experimental.pallas import tpu as pltpu
from jax.sharding import PartitionSpec as P

MESH = pl.DeviceIdType.MESH
F32 = jnp.float32
BF16 = jnp.bfloat16
HIGHEST = lax.Precision.HIGHEST

DH = 128
TOK = 128
HW = 256
KD = 1024
NW = 384
CH = 32
SH = 64
DELTAS = (1, 3, 2)
ORDER = (
    ("S", 0), ("S", 1), ("S", 2), ("S", 3), ("L",), ("T", 0, 0),
    ("U", 0, 0), ("T", 1, 0), ("U", 1, 0), ("T", 2, 0), ("U", 2, 0), ("T", 3, 0),
    ("U", 3, 0), ("T", 0, 1), ("U", 0, 1), ("T", 1, 1), ("U", 1, 1), ("T", 2, 1),
    ("U", 2, 1), ("T", 3, 1), ("U", 3, 1), ("T", 0, 2), ("U", 0, 2), ("T", 1, 2),
    ("U", 1, 2), ("T", 2, 2), ("U", 2, 2), ("T", 3, 2), ("U", 3, 2), ("T", 0, 3),
    ("U", 0, 3), ("T", 1, 3), ("U", 1, 3), ("T", 2, 3), ("U", 2, 3), ("T", 3, 3),
    ("U", 3, 3),
)


def dot(a, b, dims=((1,), (0,)), precision=None):
    return lax.dot_general(
        a, b, (dims, ((), ())), precision=precision, preferred_element_type=F32
    )


def kernel(
    k_hbm, v_hbm, q_hbm, g_hbm, decay_hbm, docs_hbm, gain_hbm, w_hbm, out_hbm,
    rx, pk, docs, gain, pkx, kf, att, abuf, wbuf, st_out, st_in,
    part, longs, shorts, total,
    go, lsem, a2a_s, a2a_r, qg_s, qg_r, pk_s, pk_r, w_s, w_r, wr_s, wr_r, st_sem,
    ag_s, ag_r, l_s, l_r, s_s, s_r, fin_s, fin_r,
):
    c, z, p = lax.axis_index("ctx"), lax.axis_index("head"), lax.axis_index("pipe")
    x, y = lax.rem(c, 4), lax.div(c, 4)

    def at_x(d):
        return 4 * y + lax.rem(x + d, 4)

    def at_y(d):
        return 4 * lax.rem(y + d, 4) + x

    def at_z(d):
        return lax.rem(z + d + 8, 8)

    def block(i, size):
        return pl.ds(pl.multiple_of(i * size, size), size)

    def remote(src, dst, send, recv, dev):
        return pltpu.make_async_remote_copy(
            src_ref=src, dst_ref=dst, send_sem=send, recv_sem=recv,
            device_id=dev, device_id_type=MESH,
        )

    def arrived(dst, recv):
        remote(dst, dst, recv, recv, (c, z, 1 - p)).wait_recv()

    sent = []

    def send(*a):
        copy = remote(*a)
        copy.start()
        sent.append(copy)

    local = [
        pltpu.make_async_copy(src, dst, lsem.at[i])
        for i, (src, dst) in enumerate(
            [
                (ref.at[0, :, block(x, HW)], rx.at[a, x])
                for a, ref in enumerate((k_hbm, v_hbm, q_hbm, g_hbm))
            ]
            + [
                (decay_hbm, pk.at[0:8, :]),
                (docs_hbm, docs),
                (gain_hbm.at[:, block(x, HW)], gain),
                (w_hbm.at[0], wbuf.at[0]),
            ]
        )
    ]
    for i in (4, 5, 6, 0, 1, 2, 3, 7):
        local[i].start()

    yo, half = lax.div(z, 2), lax.rem(z, 2)

    def fin_dev(i):
        return (4 * y + 2 * half + i, 2 * yo + lax.div(x, 2), 1 - p)

    barrier = pltpu.get_barrier_semaphore()
    peers = [(at_x(d), z, p) for d in DELTAS]
    peers += [(at_y(1), z, p), (at_y(3), z, p)]
    peers += [(c, at_z(1), p), (c, at_z(-1), p)]
    peers += [fin_dev(0), fin_dev(1)]
    peers.append((c, z, 1 - p))
    for dev in peers:
        pl.semaphore_signal(barrier, inc=1, device_id=dev, device_id_type=MESH)
    local[4].wait()
    local[5].wait()
    pk[8:16, :] = jnp.broadcast_to(docs[...].astype(F32), (8, TOK))
    pl.semaphore_wait(barrier, len(peers))

    for i, d in enumerate(DELTAS):
        send(pk, pkx.at[x], pk_s.at[i], pk_r.at[i], (at_x(d), z, p))

    def a2a(a, ref):
        for i, d in enumerate(DELTAS):
            to = lax.rem(x + d, 4)
            send(
                ref.at[0, :, block(to, HW)], rx.at[a, x],
                a2a_s.at[a, i], a2a_r.at[a, i], (at_x(d), z, p),
            )

    def a2a_wait(a):
        local[a].wait()
        for i, d in enumerate(DELTAS):
            arrived(rx.at[a, lax.rem(x + 4 - d, 4)], a2a_r.at[a, i])

    def qg_send(j):
        rr = pl.ds(j * CH, CH)
        for a, ref in enumerate((q_hbm, g_hbm)):
            for i, d in enumerate(DELTAS):
                to = lax.rem(x + d, 4)
                remote(
                    ref.at[0, rr, block(to, HW)], rx.at[2 + a, x, rr, :],
                    qg_s.at[a, i, j], qg_r.at[a, i, j], (at_x(d), z, p),
                ).start()

    def qg_wait(a, j):
        for i, d in enumerate(DELTAS):
            src = lax.rem(x + 4 - d, 4)
            arrived(rx.at[2 + a, src, pl.ds(j * CH, CH), :], qg_r.at[a, i, j])

    def w_copy(side, ch):
        rows = pl.ds(ch * HW, HW)
        return remote(
            w_hbm.at[0, rows, :], wbuf.at[(3, 1)[side], rows, :],
            w_s.at[side, ch], w_r.at[side, ch], (at_y((1, 3)[side]), z, p),
        )

    def w_wait(side, ch):
        arrived(wbuf.at[(3, 1)[side], pl.ds(ch * HW, HW), :], w_r.at[side, ch])

    def w_relay_copy(side, ch):
        rows = pl.ds(ch * HW, HW)
        return remote(
            wbuf.at[(3, 1)[side], rows, :], wbuf.at[2, rows, :],
            wr_s.at[ch], wr_r.at[ch], (at_y((1, 3)[side]), z, p),
        )

    def weights(core, chunks):
        @pl.when(p == core)
        def _():
            for side, ch in chunks:
                w_copy(side, ch).start()

    def relays(core):
        @pl.when(p == core)
        def _():
            for ch in range(2):
                for side, i in ((0, ch), (1, 2 + ch)):
                    w_wait(side, i)
                    w_relay_copy(side, i).start()

    @pl.when(p == 0)
    def _():
        pl.semaphore_wait(go, 1)

    a2a(0, k_hbm)
    a2a(1, v_hbm)
    weights(1, ((0, 0), (1, 2), (0, 1), (1, 3)))
    for j in range(3):
        qg_send(j)

    @pl.when(p == 1)
    def _():
        qg_send(3)

    weights(1, ((1, 0), (0, 2), (1, 1)))

    i8 = lax.broadcasted_iota(jnp.int32, (8, 8), 0)
    j8 = lax.broadcasted_iota(jnp.int32, (8, 8), 1)
    pick = (j8 == 2 * x + i8).astype(F32)
    ia = lax.broadcasted_iota(jnp.int32, (TOK, TOK), 0)
    ib = lax.broadcasted_iota(jnp.int32, (TOK, TOK), 1)
    upper = (ia <= ib).astype(F32)
    lower = (ia >= ib).astype(F32)
    eye = (ia == ib).astype(F32)
    for i, d in enumerate(DELTAS):
        arrived(pkx.at[lax.rem(x + 4 - d, 4)], pk_r.at[i])
    pkx[x] = pk[...]
    rows_, cols_, segr, segc = [], [], [], []
    off_r, off_c = jnp.zeros((8, 1), F32), jnp.zeros((1, 8), F32)
    for b in range(4):
        two = dot(pick, pkx[b, 0:8, :], precision=HIGHEST)
        r = dot(two, upper, precision=HIGHEST) + off_r
        s = dot(lower, two, ((1,), (1,)), precision=HIGHEST) + off_c
        e = dot(eye, pkx[b, 8:16, :], ((1,), (1,)), precision=HIGHEST)
        off_r, off_c = r[:, TOK - 1 : TOK], s[TOK - 1 : TOK, :]
        rows_.append(r)
        cols_.append(s)
        segr.append(pkx[b, 8:9, :])
        segc.append(e[:, 0:1])
    last_doc = segr[3][:, TOK - 1 : TOK]

    weights(0, ((1, 2), (1, 3)))
    a2a_wait(0)
    a2a_wait(1)

    @pl.when(p == 1)
    def _():
        pl.semaphore_signal(go, inc=1, device_id=(c, z, 0), device_id_type=MESH)

    for b in range(4):
        keep = (segc[b] == last_doc).astype(F32)
        for h in range(2):
            hs = slice(h, h + 1)
            hh = slice(h * DH, (h + 1) * DH)
            fade = jnp.exp(jnp.minimum(off_c[:, hs] - cols_[b][:, hs], 0.0)) * keep
            kf[b * TOK : (b + 1) * TOK, hh] = (rx[0, b, :, hh].astype(F32) * fade).astype(BF16)
    for h in range(2):
        hh = slice(h * DH, (h + 1) * DH)
        values = rx[1, :, :, hh].reshape(4 * TOK, DH)
        st_out[hh, :] = dot(kf[:, hh], values, ((0,), (0,))).astype(BF16)
    st_out[256:272, :] = jnp.broadcast_to(last_doc, (16, DH)).astype(BF16)
    send(st_out, st_in, st_sem.at[0], st_sem.at[1], (at_y(1), z, p))
    weights(1, ((0, 3),))
    relays(1)
    weights(0, ((0, 0), (0, 1), (0, 2), (1, 0), (0, 3), (1, 1)))

    base = lax.broadcasted_iota(jnp.int32, (TOK, 4 * TOK), 0)
    base = lax.shift_right_logical(base, 5) * TOK + (base & (CH - 1))
    ahead = lax.broadcasted_iota(jnp.int32, (TOK, 4 * TOK), 1) - base
    seg_row = jnp.concatenate(segr, axis=1)
    crow = [jnp.concatenate([r[h : h + 1, :] for r in rows_], axis=1) for h in range(2)]
    later = (y > 0).astype(F32)

    def inside(j):
        rr = slice(j * CH, (j + 1) * CH)
        seg_t = jnp.concatenate([e[rr, :] for e in segc], axis=0)
        allowed = (ahead <= j * CH) & (seg_t == seg_row)
        for h in range(2):
            hh = slice(h * DH, (h + 1) * DH)
            ccol = jnp.concatenate([s[rr, h : h + 1] for s in cols_], axis=0)
            weight = jnp.where(allowed, jnp.exp(jnp.minimum(ccol - crow[h], 0.0)), 0.0)
            queries = rx[2, :, rr, hh].reshape(TOK, DH)
            scores = dot(queries, rx[0, :, :, hh].reshape(4 * TOK, DH), ((1,), (1,)))
            mixed = (scores * weight).astype(BF16)
            att[j, :, hh] = dot(mixed, rx[1, :, :, hh].reshape(4 * TOK, DH))

    def finish(j):
        rr = slice(j * CH, (j + 1) * CH)
        prev_doc = st_in[256:257, 0:1].astype(F32)
        seg_t = jnp.concatenate([e[rr, :] for e in segc], axis=0)
        same = (seg_t == prev_doc).astype(F32) * later
        for h in range(2):
            hh = slice(h * DH, (h + 1) * DH)
            ccol = jnp.concatenate([s[rr, h : h + 1] for s in cols_], axis=0)
            queries = rx[2, :, rr, hh].reshape(TOK, DH)
            full = att[j, :, hh] + dot(queries, st_in[hh, :]) * (jnp.exp(ccol) * same)
            scale = lax.rsqrt(jnp.mean(full * full, axis=-1, keepdims=True) + 1e-06)
            gates = rx[3, :, rr, hh].reshape(TOK, DH).astype(F32)
            normed = full * scale * gain[:, hh] * (1.0 / (1.0 + jnp.exp(-gates)))
            abuf[0, :, rr, hh] = normed.astype(BF16).reshape(4, CH, DH)
        for i, d in enumerate(DELTAS):
            rr = pl.ds(j * CH, CH)
            send(
                abuf.at[0, :, rr, :], abuf.at[1 + i, :, rr, :],
                ag_s.at[i, j], ag_r.at[i, j], (at_x(d), z, p),
            )

    local[2].wait()
    local[3].wait()
    local[6].wait()
    for j in range(4):
        qg_wait(0, j)
        inside(j)
        qg_wait(1, j)
        if j == 0:
            arrived(st_in, st_sem.at[1])
        finish(j)
        if j == 0:

            @pl.when(p == 0)
            def _():
                qg_send(3)

        if j == 2:
            relays(0)
    xs = [lax.rem(x + d, 4) for d in (0, 3, 1, 2)]
    local[7].wait()

    def project(j):
        for i in range(3):
            arrived(abuf.at[1 + i, :, pl.ds(j * CH, CH), :], ag_r.at[i, j])
        if j == 0:
            for ch in range(2):
                w_wait(0, 2 + ch)
                w_wait(1, ch)

        def body(n, carry):
            d = n + lax.div(n, 2)
            acc = jnp.zeros((4 * CH, NW), F32)
            for s in range(4):
                lhs = abuf[s, :, j * CH : (j + 1) * CH, :].reshape(4 * CH, HW)
                acc = acc + dot(lhs, wbuf[d, block(xs[s], HW), :])
            acc = acc.astype(BF16)
            yy = lax.rem(y + d, 4)
            part[j, 2 * yy] = acc[:SH, :]
            part[j, 2 * yy + 1] = acc[SH:, :]
            return carry

        lax.fori_loop(0, 3, body, 0)

    def project_late():
        for ch in range(4):
            arrived(wbuf.at[2, pl.ds(ch * HW, HW), :], wr_r.at[ch])
        yy = lax.rem(y + 2, 4)

        def body(n, carry):
            for i in range(2):
                acc = jnp.zeros((TOK, NW), F32)
                for s in range(4):
                    acc = acc + dot(abuf[s, 2 * n + i], wbuf[2, block(xs[s], HW), :])
                acc = acc.astype(BF16)
                for j in range(4):
                    part[j, 2 * yy + n, i * CH : (i + 1) * CH, :] = acc[j * CH : (j + 1) * CH, :]
            return carry

        lax.fori_loop(0, 2, body, 0)

    def owner(k):
        return lax.rem(z + k + 16, 8)

    def is_late(o):
        return lax.rem(lax.div(o, 2) - y + 4, 4) == 2

    def when(o, late):
        return pl.when(is_late(o) if late else jnp.logical_not(is_late(o)))

    def sign(j):
        return (1, -1)[j % 2]

    def long_copy(src, j, t):
        return remote(
            src, longs.at[j, t], l_s.at[j, t], l_r.at[j, t], (c, at_z(-sign(j)), p)
        )

    def short_copy(src, j, t):
        return remote(
            src, shorts.at[j, t], s_s.at[j, t], s_r.at[j, t], (c, at_z(sign(j)), p)
        )

    def start(j, late):
        s = sign(j)
        lo, so = owner(-4 * s), owner(3 * s)

        @when(lo, late)
        def _():
            long_copy(part.at[j, lo], j, 0).start()

        @when(so, late)
        def _():
            short_copy(part.at[j, so], j, 0).start()

    def fin_copy(j, i):
        return remote(
            total.at[j, pl.ds(i * CH, CH), :],
            out_hbm.at[0, pl.ds(j * CH, CH), block(lax.rem(x, 2), NW)],
            fin_s.at[j, i], fin_r.at[j, lax.rem(x, 2)], fin_dev(i),
        )

    def step(j, t, late):
        s = sign(j)
        lo, so = owner(-s * (3 - t)), owner(s * (2 - t))

        @when(lo, late)
        def _():
            arrived(longs.at[j, t], l_r.at[j, t])
            mine = longs[j, t].astype(F32) + part[j, lo].astype(F32)
            if t < 3:
                longs[j, t] = mine.astype(BF16)
                long_copy(longs.at[j, t], j, t + 1).start()
            else:
                arrived(shorts.at[j, 2], s_r.at[j, 2])
                total[j] = (mine + shorts[j, 2].astype(F32)).astype(BF16)
                for i in range(2):
                    fin_copy(j, i).start()

        if t < 2:

            @when(so, late)
            def _():
                arrived(shorts.at[j, t], s_r.at[j, t])
                mine = shorts[j, t].astype(F32) + part[j, so].astype(F32)
                shorts[j, t] = mine.astype(BF16)
                short_copy(shorts.at[j, t], j, t + 1).start()

    for op in ORDER:
        if op[0] == "S":
            project(op[1])
            start(op[1], False)
        elif op[0] == "L":
            project_late()
            for j in range(4):
                start(j, True)
        else:
            step(op[1], op[2], op[0] == "U")

    for j in range(4):
        for xx in range(2):
            arrived(
                out_hbm.at[0, pl.ds(j * CH, CH), pl.ds(xx * NW, NW)], fin_r.at[j, xx]
            )
        for t in range(4):
            long_copy(longs.at[j, t], j, t).wait_send()
        for t in range(3):
            short_copy(shorts.at[j, t], j, t).wait_send()
        for i in range(2):
            fin_copy(j, i).wait_send()
    for ch in range(4):
        for side in range(2):
            w_copy(side, ch).wait_send()
        w_relay_copy((0, 0, 1, 1)[ch], ch).wait_send()
    for j in range(4):
        for i in range(3):
            for a in range(2):
                rr = rx.at[2 + a, x, pl.ds(j * CH, CH), :]
                remote(rr, rr, qg_s.at[a, i, j], qg_r.at[a, i, j], (c, z, 1 - p)).wait_send()
    for copy in sent:
        copy.wait_send()


def on_device(queries, keys, values, gates, log_decay, segment_ids, norm_gain, out_weight):
    hbm = pl.BlockSpec(memory_space=pltpu.HBM)
    vmem = pltpu.VMEM
    dma = pltpu.SemaphoreType.DMA
    return pl.pallas_call(
        kernel,
        out_shape=jax.ShapeDtypeStruct((1, TOK, 2 * NW), BF16),
        in_specs=[hbm] * 8,
        out_specs=hbm,
        scratch_shapes=[
            vmem((4, 4, TOK, HW), BF16),
            vmem((16, TOK), F32),
            vmem((1, TOK), jnp.int32),
            vmem((1, HW), F32),
            vmem((4, 16, TOK), F32),
            vmem((4 * TOK, HW), BF16),
            vmem((4, TOK, HW), F32),
            vmem((4, 4, TOK, HW), BF16),
            vmem((4, KD, NW), BF16),
            vmem((272, DH), BF16),
            vmem((272, DH), BF16),
            vmem((4, 8, SH, NW), BF16),
            vmem((4, 4, SH, NW), BF16),
            vmem((4, 3, SH, NW), BF16),
            vmem((4, SH, NW), BF16),
            pltpu.SemaphoreType.REGULAR, dma((8,)), dma((2, 3)), dma((2, 3)), dma((2, 3, 4)), dma((2, 3, 4)),
            dma((3,)), dma((3,)),
            dma((2, 4)), dma((2, 4)), dma((4,)), dma((4,)), dma((2,)),
            dma((3, 4)), dma((3, 4)),
            dma((4, 4)), dma((4, 4)), dma((4, 3)), dma((4, 3)),
            dma((4, 2)), dma((4, 2)),
        ],
        compiler_params=pltpu.CompilerParams(
            collective_id=0, has_side_effects=True, vmem_limit_bytes=60 * 2**20
        ),
        cost_estimate=pl.CostEstimate(
            flops=2 * 10**9, bytes_accessed=3 * 2**20, transcendentals=10**6
        ),
    )(
        keys, values, queries, gates, log_decay[0].T, segment_ids, norm_gain, out_weight
    )


def solution(mesh):
    return jax.shard_map(
        on_device,
        mesh=mesh,
        in_specs=(
            P("pipe", "ctx", "head"),
            P("pipe", "ctx", "head"),
            P("pipe", "ctx", "head"),
            P("pipe", "ctx", "head"),
            P("pipe", "ctx", "head"),
            P("pipe", "ctx"),
            P("pipe", "head"),
            P("pipe", "head", "ctx"),
        ),
        out_specs=P("pipe", "ctx", "head"),
        check_vma=False,
    )
```

time: 72.8 us -> 60.7 us (0.83)
  the two profiles are of different devices: /device:TPU:23 before, /device:TPU:33 now
where the time goes in v3:
time: 60.7 us; the launch traced here: 60.6 us
  Pallas kernels  59 us (97%)
  local copies, waits for them, and re-layouts  1.62 us (3%)
    pallas_call x1, Pallas kernels, on_device(): pl.pallas_call(kernel, out_shape=jax.ShapeDtypeStruct((1, TOK, 2 * NW), B...  59 us
    unnamed x1, local copies, waits for them, and re-layouts  1.62 us

profile of v3, /device:TPU:33, one launch (start us, length us, event | category | flops | bytes accessed | tf_op | source)
XLA Modules:
  0.0 60.6 jit_solution(6646677835182059934)
XLA Ops:
  0.0 59.0 %shard_map.82 = bf16[1,128,768]{2,1,0:T(8,128)(2,1)} custom-call(bf16[1,128,1024]{2,1,0:T(8,128)(2,1)} %k_hbm.1, bf16[1,128,1024]{2,1,0:T(8,128)(2,1)} %v_hbm.1, bf16[1,128,1024]{2,1,0:T(8,128)(2,1)} %q_hbm.1, bf16[1,128,1024]{2,1,0:T(8,128)(2,1)} %g_hbm.1, f32[8,128]{1,0:T(8,128)} %bitcast.3, s32[1,128]{1,0:T(1,128)} %docs_hbm.1, f32[1,1024]{1,0:T(1,128)} %gain_hbm.1, ...), custom_call_target="tpu_custom_call" | custom-call | flops 2000000000 | bytes 3145728 | tf_op jit(solution)/shard_map/pallas_call | solution.py:447
  59.0 1.6 %copy.10 = bf16[1,128,768]{2,1,0:T(8,128)(2,1)} copy(bf16[1,128,768]{2,1,0:T(8,128)(2,1)} %shard_map.82) | data formatting | bytes 393216

commit v4 on v3

--- a/solution.py
+++ b/solution.py
@@ -39,7 +39,7 @@
     k_hbm, v_hbm, q_hbm, g_hbm, decay_hbm, docs_hbm, gain_hbm, w_hbm, out_hbm,
     rx, pk, docs, gain, pkx, kf, att, abuf, wbuf, st_out, st_in,
     part, longs, shorts, total,
-    go, lsem, a2a_s, a2a_r, qg_s, qg_r, pk_s, pk_r, w_s, w_r, wr_s, wr_r, st_sem,
+    go, lsem, a2a_s, a2a_r, pk_s, pk_r, w_s, w_r, wr_s, wr_r, st_sem,
     ag_s, ag_r, l_s, l_r, s_s, s_r, fin_s, fin_r,
 ):
     c, z, p = lax.axis_index("ctx"), lax.axis_index("head"), lax.axis_index("pipe")
@@ -66,12 +66,11 @@
     def arrived(dst, recv):
         remote(dst, dst, recv, recv, (c, z, 1 - p)).wait_recv()
 
-    sent = []
-
     def send(*a):
-        copy = remote(*a)
-        copy.start()
-        sent.append(copy)
+        remote(*a).start()
+
+    def all_sent(ref, sem):
+        remote(ref, ref, sem, sem, (c, z, 1 - p)).wait_send()
 
     local = [
         pltpu.make_async_copy(src, dst, lsem.at[i])
@@ -110,51 +109,33 @@
     pl.semaphore_wait(barrier, len(peers))
 
     for i, d in enumerate(DELTAS):
-        send(pk, pkx.at[x], pk_s.at[i], pk_r.at[i], (at_x(d), z, p))
+        send(pk, pkx.at[x], pk_s, pk_r, (at_x(d), z, p))
 
     def a2a(a, ref):
         for i, d in enumerate(DELTAS):
             to = lax.rem(x + d, 4)
             send(
                 ref.at[0, :, block(to, HW)], rx.at[a, x],
-                a2a_s.at[a, i], a2a_r.at[a, i], (at_x(d), z, p),
+                a2a_s, a2a_r.at[a], (at_x(d), z, p),
             )
 
     def a2a_wait(a):
         local[a].wait()
-        for i, d in enumerate(DELTAS):
-            arrived(rx.at[a, lax.rem(x + 4 - d, 4)], a2a_r.at[a, i])
-
-    def qg_send(j):
-        rr = pl.ds(j * CH, CH)
-        for a, ref in enumerate((q_hbm, g_hbm)):
-            for i, d in enumerate(DELTAS):
-                to = lax.rem(x + d, 4)
-                remote(
-                    ref.at[0, rr, block(to, HW)], rx.at[2 + a, x, rr, :],
-                    qg_s.at[a, i, j], qg_r.at[a, i, j], (at_x(d), z, p),
-                ).start()
-
-    def qg_wait(a, j):
-        for i, d in enumerate(DELTAS):
-            src = lax.rem(x + 4 - d, 4)
-            arrived(rx.at[2 + a, src, pl.ds(j * CH, CH), :], qg_r.at[a, i, j])
+        arrived(rx.at[a, 0:3], a2a_r.at[a])
 
     def w_copy(side, ch):
         rows = pl.ds(ch * HW, HW)
+        first = (ch < 2) == (side == 0)
         return remote(
             w_hbm.at[0, rows, :], wbuf.at[(3, 1)[side], rows, :],
-            w_s.at[side, ch], w_r.at[side, ch], (at_y((1, 3)[side]), z, p),
-        )
-
-    def w_wait(side, ch):
-        arrived(wbuf.at[(3, 1)[side], pl.ds(ch * HW, HW), :], w_r.at[side, ch])
+            w_s, w_r.at[ch if first else 4], (at_y((1, 3)[side]), z, p),
+        )
 
     def w_relay_copy(side, ch):
         rows = pl.ds(ch * HW, HW)
         return remote(
             wbuf.at[(3, 1)[side], rows, :], wbuf.at[2, rows, :],
-            wr_s.at[ch], wr_r.at[ch], (at_y((1, 3)[side]), z, p),
+            wr_s, wr_r, (at_y((1, 3)[side]), z, p),
         )
 
     def weights(core, chunks):
@@ -168,7 +149,7 @@
         def _():
             for ch in range(2):
                 for side, i in ((0, ch), (1, 2 + ch)):
-                    w_wait(side, i)
+                    arrived(wbuf.at[(3, 1)[side], pl.ds(i * HW, HW), :], w_r.at[i])
                     w_relay_copy(side, i).start()
 
     @pl.when(p == 0)
@@ -178,13 +159,8 @@
     a2a(0, k_hbm)
     a2a(1, v_hbm)
     weights(1, ((0, 0), (1, 2), (0, 1), (1, 3)))
-    for j in range(3):
-        qg_send(j)
-
-    @pl.when(p == 1)
-    def _():
-        qg_send(3)
-
+    a2a(2, q_hbm)
+    a2a(3, g_hbm)
     weights(1, ((1, 0), (0, 2), (1, 1)))
 
     i8 = lax.broadcasted_iota(jnp.int32, (8, 8), 0)
@@ -195,8 +171,7 @@
     upper = (ia <= ib).astype(F32)
     lower = (ia >= ib).astype(F32)
     eye = (ia == ib).astype(F32)
-    for i, d in enumerate(DELTAS):
-        arrived(pkx.at[lax.rem(x + 4 - d, 4)], pk_r.at[i])
+    arrived(pkx.at[0:3], pk_r)
     pkx[x] = pk[...]
     rows_, cols_, segr, segc = [], [], [], []
     off_r, off_c = jnp.zeros((8, 1), F32), jnp.zeros((1, 8), F32)
@@ -275,37 +250,27 @@
             rr = pl.ds(j * CH, CH)
             send(
                 abuf.at[0, :, rr, :], abuf.at[1 + i, :, rr, :],
-                ag_s.at[i, j], ag_r.at[i, j], (at_x(d), z, p),
+                ag_s, ag_r.at[j], (at_x(d), z, p),
             )
 
-    local[2].wait()
-    local[3].wait()
+    a2a_wait(2)
     local[6].wait()
     for j in range(4):
-        qg_wait(0, j)
         inside(j)
-        qg_wait(1, j)
         if j == 0:
+            a2a_wait(3)
             arrived(st_in, st_sem.at[1])
         finish(j)
-        if j == 0:
-
-            @pl.when(p == 0)
-            def _():
-                qg_send(3)
-
         if j == 2:
             relays(0)
+
     xs = [lax.rem(x + d, 4) for d in (0, 3, 1, 2)]
     local[7].wait()
 
     def project(j):
-        for i in range(3):
-            arrived(abuf.at[1 + i, :, pl.ds(j * CH, CH), :], ag_r.at[i, j])
+        arrived(abuf.at[1:4, :, pl.ds(j * CH, CH), :], ag_r.at[j])
         if j == 0:
-            for ch in range(2):
-                w_wait(0, 2 + ch)
-                w_wait(1, ch)
+            arrived(wbuf.at[1], w_r.at[4])
 
         def body(n, carry):
             d = n + lax.div(n, 2)
@@ -322,8 +287,7 @@
         lax.fori_loop(0, 3, body, 0)
 
     def project_late():
-        for ch in range(4):
-            arrived(wbuf.at[2, pl.ds(ch * HW, HW), :], wr_r.at[ch])
+        arrived(wbuf.at[2], wr_r)
         yy = lax.rem(y + 2, 4)
 
         def body(n, carry):
@@ -352,12 +316,12 @@
 
     def long_copy(src, j, t):
         return remote(
-            src, longs.at[j, t], l_s.at[j, t], l_r.at[j, t], (c, at_z(-sign(j)), p)
+            src, longs.at[j, t], l_s, l_r.at[j, t], (c, at_z(-sign(j)), p)
         )
 
     def short_copy(src, j, t):
         return remote(
-            src, shorts.at[j, t], s_s.at[j, t], s_r.at[j, t], (c, at_z(sign(j)), p)
+            src, shorts.at[j, t], s_s, s_r.at[j, t], (c, at_z(sign(j)), p)
         )
 
     def start(j, late):
@@ -376,7 +340,7 @@
         return remote(
             total.at[j, pl.ds(i * CH, CH), :],
             out_hbm.at[0, pl.ds(j * CH, CH), block(lax.rem(x, 2), NW)],
-            fin_s.at[j, i], fin_r.at[j, lax.rem(x, 2)], fin_dev(i),
+            fin_s, fin_r, fin_dev(i),
         )
 
     def step(j, t, late):
@@ -416,28 +380,16 @@
         else:
             step(op[1], op[2], op[0] == "U")
 
-    for j in range(4):
-        for xx in range(2):
-            arrived(
-                out_hbm.at[0, pl.ds(j * CH, CH), pl.ds(xx * NW, NW)], fin_r.at[j, xx]
-            )
-        for t in range(4):
-            long_copy(longs.at[j, t], j, t).wait_send()
-        for t in range(3):
-            short_copy(shorts.at[j, t], j, t).wait_send()
-        for i in range(2):
-            fin_copy(j, i).wait_send()
-    for ch in range(4):
-        for side in range(2):
-            w_copy(side, ch).wait_send()
-        w_relay_copy((0, 0, 1, 1)[ch], ch).wait_send()
-    for j in range(4):
-        for i in range(3):
-            for a in range(2):
-                rr = rx.at[2 + a, x, pl.ds(j * CH, CH), :]
-                remote(rr, rr, qg_s.at[a, i, j], qg_r.at[a, i, j], (c, z, 1 - p)).wait_send()
-    for copy in sent:
-        copy.wait_send()
+    arrived(out_hbm.at[0], fin_r)
+    all_sent(pkx.at[0:3], pk_s)
+    all_sent(rx.at[0:3], a2a_s)
+    all_sent(wbuf.at[0:2], w_s)
+    all_sent(wbuf.at[2], wr_s)
+    all_sent(st_out, st_sem.at[0])
+    all_sent(abuf.at[0:3], ag_s)
+    all_sent(longs, l_s)
+    all_sent(shorts, s_s)
+    all_sent(total, fin_s)
 
 
 def on_device(queries, keys, values, gates, log_decay, segment_ids, norm_gain, out_weight):
@@ -465,12 +417,9 @@
             vmem((4, 4, SH, NW), BF16),
             vmem((4, 3, SH, NW), BF16),
             vmem((4, SH, NW), BF16),
-            pltpu.SemaphoreType.REGULAR, dma((8,)), dma((2, 3)), dma((2, 3)), dma((2, 3, 4)), dma((2, 3, 4)),
-            dma((3,)), dma((3,)),
-            dma((2, 4)), dma((2, 4)), dma((4,)), dma((4,)), dma((2,)),
-            dma((3, 4)), dma((3, 4)),
-            dma((4, 4)), dma((4, 4)), dma((4, 3)), dma((4, 3)),
-            dma((4, 2)), dma((4, 2)),
+            pltpu.SemaphoreType.REGULAR, dma((8,)), dma, dma((4,)), dma, dma,
+            dma, dma((5,)), dma, dma, dma((2,)), dma, dma((4,)),
+            dma, dma((4, 4)), dma, dma((4, 3)), dma, dma,
         ],
         compiler_params=pltpu.CompilerParams(
             collective_id=0, has_side_effects=True, vmem_limit_bytes=60 * 2**20

time: 60.7 us -> 59.4 us (0.979)
  Pallas kernels: 59 us -> 57.7 us
    pallas_call x1, Pallas kernels: 59 us -> 57.7 us  [on_device(): pl.pallas_call(kernel, out_shape=jax.ShapeDtypeStruct((1, TOK, 2 * NW), B...]
where the time goes in v4:
time: 59.4 us; the launch traced here: 59.3 us
  Pallas kernels  57.7 us (97%)
  local copies, waits for them, and re-layouts  1.62 us (3%)
    pallas_call x1, Pallas kernels, on_device(): pl.pallas_call(kernel, out_shape=jax.ShapeDtypeStruct((1, TOK, 2 * NW), B...  57.7 us
    unnamed x1, local copies, waits for them, and re-layouts  1.62 us

profile of v4, /device:TPU:33, one launch (start us, length us, event | category | flops | bytes accessed | tf_op | source)
XLA Modules:
  0.0 59.3 jit_solution(11777622553745527231)
XLA Ops:
  0.0 57.7 %shard_map.82 = bf16[1,128,768]{2,1,0:T(8,128)(2,1)} custom-call(bf16[1,128,1024]{2,1,0:T(8,128)(2,1)} %k_hbm.1, bf16[1,128,1024]{2,1,0:T(8,128)(2,1)} %v_hbm.1, bf16[1,128,1024]{2,1,0:T(8,128)(2,1)} %q_hbm.1, bf16[1,128,1024]{2,1,0:T(8,128)(2,1)} %g_hbm.1, f32[8,128]{1,0:T(8,128)} %bitcast.3, s32[1,128]{1,0:T(1,128)} %docs_hbm.1, f32[1,1024]{1,0:T(1,128)} %gain_hbm.1, ...), custom_call_target="tpu_custom_call" | custom-call | flops 2000000000 | bytes 3145728 | tf_op jit(solution)/shard_map/pallas_call | solution.py:399
  57.7 1.6 %copy.10 = bf16[1,128,768]{2,1,0:T(8,128)(2,1)} copy(bf16[1,128,768]{2,1,0:T(8,128)(2,1)} %shard_map.82) | data formatting | bytes 393216

commit v5 on v4

--- a/solution.py
+++ b/solution.py
@@ -18,15 +18,8 @@
 CH = 32
 SH = 64
 DELTAS = (1, 3, 2)
-ORDER = (
-    ("S", 0), ("S", 1), ("S", 2), ("S", 3), ("L",), ("T", 0, 0),
-    ("U", 0, 0), ("T", 1, 0), ("U", 1, 0), ("T", 2, 0), ("U", 2, 0), ("T", 3, 0),
-    ("U", 3, 0), ("T", 0, 1), ("U", 0, 1), ("T", 1, 1), ("U", 1, 1), ("T", 2, 1),
-    ("U", 2, 1), ("T", 3, 1), ("U", 3, 1), ("T", 0, 2), ("U", 0, 2), ("T", 1, 2),
-    ("U", 1, 2), ("T", 2, 2), ("U", 2, 2), ("T", 3, 2), ("U", 3, 2), ("T", 0, 3),
-    ("U", 0, 3), ("T", 1, 3), ("U", 1, 3), ("T", 2, 3), ("U", 2, 3), ("T", 3, 3),
-    ("U", 3, 3),
-)
+
+EARLY = ((), ((0, 0),), ((1, 0),), ((2, 0), (0, 1)))
 
 
 def dot(a, b, dims=((1,), (0,)), precision=None):
@@ -38,9 +31,9 @@
 def kernel(
     k_hbm, v_hbm, q_hbm, g_hbm, decay_hbm, docs_hbm, gain_hbm, w_hbm, out_hbm,
     rx, pk, docs, gain, pkx, kf, att, abuf, wbuf, st_out, st_in,
-    part, longs, shorts, total,
+    part, land, total,
     go, lsem, a2a_s, a2a_r, pk_s, pk_r, w_s, w_r, wr_s, wr_r, st_sem,
-    ag_s, ag_r, l_s, l_r, s_s, s_r, fin_s, fin_r,
+    ag_s, ag_r, z_s, z_r, fin_s, fin_r,
 ):
     c, z, p = lax.axis_index("ctx"), lax.axis_index("head"), lax.axis_index("pipe")
     x, y = lax.rem(c, 4), lax.div(c, 4)
@@ -98,7 +91,7 @@
     barrier = pltpu.get_barrier_semaphore()
     peers = [(at_x(d), z, p) for d in DELTAS]
     peers += [(at_y(1), z, p), (at_y(3), z, p)]
-    peers += [(c, at_z(1), p), (c, at_z(-1), p)]
+    peers += [(c, at_z(d), p) for d in (1, -1, 2, -2)]
     peers += [fin_dev(0), fin_dev(1)]
     peers.append((c, z, 1 - p))
     for dev in peers:
@@ -257,11 +250,11 @@
     local[6].wait()
     for j in range(4):
         inside(j)
-        if j == 0:
-            a2a_wait(3)
-            arrived(st_in, st_sem.at[1])
+    a2a_wait(3)
+    arrived(st_in, st_sem.at[1])
+    for j in range(4):
         finish(j)
-        if j == 2:
+        if j == 3:
             relays(0)
 
     xs = [lax.rem(x + d, 4) for d in (0, 3, 1, 2)]
@@ -314,27 +307,33 @@
     def sign(j):
         return (1, -1)[j % 2]
 
-    def long_copy(src, j, t):
+    def z_copy(src, j, slot, d):
         return remote(
-            src, longs.at[j, t], l_s, l_r.at[j, t], (c, at_z(-sign(j)), p)
-        )
-
-    def short_copy(src, j, t):
-        return remote(
-            src, shorts.at[j, t], s_s, s_r.at[j, t], (c, at_z(sign(j)), p)
-        )
+            src, land.at[j, slot], z_s, z_r.at[j, slot], (c, at_z(sign(j) * d), p)
+        )
+
+    def landed(j, slot):
+        arrived(land.at[j, slot], z_r.at[j, slot])
+        return land[j, slot].astype(F32)
+
+    def mine(j, o):
+        return part[j, o].astype(F32)
 
     def start(j, late):
-        s = sign(j)
-        lo, so = owner(-4 * s), owner(3 * s)
-
-        @when(lo, late)
-        def _():
-            long_copy(part.at[j, lo], j, 0).start()
-
-        @when(so, late)
-        def _():
-            short_copy(part.at[j, so], j, 0).start()
+        for slot, d, to in ((0, -4, -1), (4, 3, 1)):
+            o = owner(sign(j) * d)
+
+            @when(o, late)
+            def _():
+                z_copy(part.at[j, o], j, slot, to).start()
+
+    def start_short(j, late):
+        for slot, d, to in ((0, -4, -2), (1, -3, -1), (2, 3, 1), (3, -1, -1), (4, 1, 1)):
+            o = owner(sign(j) * d)
+
+            @when(o, late)
+            def _():
+                z_copy(part.at[j, o], j, slot, to).start()
 
     def fin_copy(j, i):
         return remote(
@@ -343,42 +342,88 @@
             fin_s, fin_r, fin_dev(i),
         )
 
+    def finished(j, acc):
+        total[j] = acc.astype(BF16)
+        for i in range(2):
+            fin_copy(j, i).start()
+
     def step(j, t, late):
         s = sign(j)
         lo, so = owner(-s * (3 - t)), owner(s * (2 - t))
 
         @when(lo, late)
         def _():
-            arrived(longs.at[j, t], l_r.at[j, t])
-            mine = longs[j, t].astype(F32) + part[j, lo].astype(F32)
+            acc = mine(j, lo) + landed(j, t)
             if t < 3:
-                longs[j, t] = mine.astype(BF16)
-                long_copy(longs.at[j, t], j, t + 1).start()
+                land[j, t] = acc.astype(BF16)
+                z_copy(land.at[j, t], j, t + 1, -1).start()
             else:
-                arrived(shorts.at[j, 2], s_r.at[j, 2])
-                total[j] = (mine + shorts[j, 2].astype(F32)).astype(BF16)
-                for i in range(2):
-                    fin_copy(j, i).start()
+                finished(j, acc + landed(j, 6))
 
         if t < 2:
 
             @when(so, late)
             def _():
-                arrived(shorts.at[j, t], s_r.at[j, t])
-                mine = shorts[j, t].astype(F32) + part[j, so].astype(F32)
-                shorts[j, t] = mine.astype(BF16)
-                short_copy(shorts.at[j, t], j, t + 1).start()
-
-    for op in ORDER:
-        if op[0] == "S":
-            project(op[1])
-            start(op[1], False)
-        elif op[0] == "L":
-            project_late()
+                land[j, 4 + t] = (mine(j, so) + landed(j, 4 + t)).astype(BF16)
+                z_copy(land.at[j, 4 + t], j, 5 + t, 1).start()
+
+    def middle(j, late):
+        lo, so = owner(-2 * sign(j)), owner(2 * sign(j))
+
+        @when(lo, late)
+        def _():
+            land[j, 0] = (mine(j, lo) + landed(j, 0) + landed(j, 1)).astype(BF16)
+            z_copy(land.at[j, 0], j, 5, -2).start()
+
+        @when(so, late)
+        def _():
+            land[j, 2] = (mine(j, so) + landed(j, 2)).astype(BF16)
+            z_copy(land.at[j, 2], j, 6, 2).start()
+
+    def end(j, late):
+        @when(owner(0), late)
+        def _():
+            acc = mine(j, z)
+            for slot in (3, 4, 5, 6):
+                acc = acc + landed(j, slot)
+            finished(j, acc)
+
+    def begin(j, late):
+        @pl.when(p == 1)
+        def _():
+            start(j, late)
+
+        @pl.when(p == 0)
+        def _():
+            start_short(j, late)
+
+    for j in range(4):
+        project(j)
+        begin(j, False)
+
+        @pl.when(p == 1)
+        def _():
+            for i, t in EARLY[j]:
+                step(i, t, False)
+
+    project_late()
+    for j in range(4):
+        begin(j, True)
+
+    @pl.when(p == 1)
+    def _():
+        for t in range(4):
             for j in range(4):
-                start(j, True)
-        else:
-            step(op[1], op[2], op[0] == "U")
+                if (j, t) not in sum(EARLY, ()):
+                    step(j, t, False)
+                step(j, t, True)
+
+    @pl.when(p == 0)
+    def _():
+        for work in (middle, end):
+            for j in range(4):
+                work(j, False)
+                work(j, True)
 
     arrived(out_hbm.at[0], fin_r)
     all_sent(pkx.at[0:3], pk_s)
@@ -387,8 +432,7 @@
     all_sent(wbuf.at[2], wr_s)
     all_sent(st_out, st_sem.at[0])
     all_sent(abuf.at[0:3], ag_s)
-    all_sent(longs, l_s)
-    all_sent(shorts, s_s)
+    all_sent(land, z_s)
     all_sent(total, fin_s)
 
 
@@ -414,12 +458,11 @@
             vmem((272, DH), BF16),
             vmem((272, DH), BF16),
             vmem((4, 8, SH, NW), BF16),
-            vmem((4, 4, SH, NW), BF16),
-            vmem((4, 3, SH, NW), BF16),
+            vmem((4, 7, SH, NW), BF16),
             vmem((4, SH, NW), BF16),
             pltpu.SemaphoreType.REGULAR, dma((8,)), dma, dma((4,)), dma, dma,
             dma, dma((5,)), dma, dma, dma((2,)), dma, dma((4,)),
-            dma, dma((4, 4)), dma, dma((4, 3)), dma, dma,
+            dma, dma((4, 7)), dma, dma,
         ],
         compiler_params=pltpu.CompilerParams(
             collective_id=0, has_side_effects=True, vmem_limit_bytes=60 * 2**20

time: 59.4 us -> 59.2 us (level)
  Pallas kernels: 57.7 us -> 57.1 us
    pallas_call x1, Pallas kernels: 57.7 us -> 57.1 us  [on_device(): pl.pallas_call(kernel, out_shape=jax.ShapeDtypeStruct((1, TOK, 2 * NW), B...]
where the time goes in v5:
time: 59.2 us; the launch traced here: 58.7 us
  Pallas kernels  57.1 us (96%)
  local copies, waits for them, and re-layouts  1.62 us (3%)
    pallas_call x1, Pallas kernels, on_device(): pl.pallas_call(kernel, out_shape=jax.ShapeDtypeStruct((1, TOK, 2 * NW), B...  57.1 us
    unnamed x1, local copies, waits for them, and re-layouts  1.62 us

profile of v5, /device:TPU:33, one launch (start us, length us, event | category | flops | bytes accessed | tf_op | source)
XLA Modules:
  0.0 58.7 jit_solution(9811128645489161044)
XLA Ops:
  0.0 57.1 %shard_map.82 = bf16[1,128,768]{2,1,0:T(8,128)(2,1)} custom-call(bf16[1,128,1024]{2,1,0:T(8,128)(2,1)} %k_hbm.1, bf16[1,128,1024]{2,1,0:T(8,128)(2,1)} %v_hbm.1, bf16[1,128,1024]{2,1,0:T(8,128)(2,1)} %q_hbm.1, bf16[1,128,1024]{2,1,0:T(8,128)(2,1)} %g_hbm.1, f32[8,128]{1,0:T(8,128)} %bitcast.3, s32[1,128]{1,0:T(1,128)} %docs_hbm.1, f32[1,1024]{1,0:T(1,128)} %gain_hbm.1, ...), custom_call_target="tpu_custom_call" | custom-call | flops 2000000000 | bytes 3145728 | tf_op jit(solution)/shard_map/pallas_call | solution.py:443
  57.1 1.6 %copy.10 = bf16[1,128,768]{2,1,0:T(8,128)(2,1)} copy(bf16[1,128,768]{2,1,0:T(8,128)(2,1)} %shard_map.82) | data formatting | bytes 393216

commit v6 on v4

--- a/solution.py
+++ b/solution.py
@@ -73,7 +73,7 @@
         remote(ref, ref, sem, sem, (c, z, 1 - p)).wait_send()
 
     local = [
-        pltpu.make_async_copy(src, dst, lsem.at[i])
+        pltpu.make_async_copy(src, dst, a2a_r.at[i] if i < 4 else lsem.at[i - 4])
         for i, (src, dst) in enumerate(
             [
                 (ref.at[0, :, block(x, HW)], rx.at[a, x])
@@ -120,8 +120,7 @@
             )
 
     def a2a_wait(a):
-        local[a].wait()
-        arrived(rx.at[a, 0:3], a2a_r.at[a])
+        arrived(rx.at[a], a2a_r.at[a])
 
     def w_copy(side, ch):
         rows = pl.ds(ch * HW, HW)
@@ -159,8 +158,11 @@
     a2a(0, k_hbm)
     a2a(1, v_hbm)
     weights(1, ((0, 0), (1, 2), (0, 1), (1, 3)))
-    a2a(2, q_hbm)
-    a2a(3, g_hbm)
+    @pl.when(p == 1)
+    def _():
+        a2a(2, q_hbm)
+        a2a(3, g_hbm)
+
     weights(1, ((1, 0), (0, 2), (1, 1)))
 
     i8 = lax.broadcasted_iota(jnp.int32, (8, 8), 0)
@@ -187,6 +189,11 @@
         segc.append(e[:, 0:1])
     last_doc = segr[3][:, TOK - 1 : TOK]
 
+    @pl.when(p == 0)
+    def _():
+        a2a(2, q_hbm)
+        a2a(3, g_hbm)
+
     weights(0, ((1, 2), (1, 3)))
     a2a_wait(0)
     a2a_wait(1)
@@ -257,12 +264,11 @@
     local[6].wait()
     for j in range(4):
         inside(j)
-        if j == 0:
-            a2a_wait(3)
-            arrived(st_in, st_sem.at[1])
+    a2a_wait(3)
+    arrived(st_in, st_sem.at[1])
+    for j in range(4):
         finish(j)
-        if j == 2:
-            relays(0)
+    relays(0)
 
     xs = [lax.rem(x + d, 4) for d in (0, 3, 1, 2)]
     local[7].wait()
@@ -417,7 +423,7 @@
             vmem((4, 4, SH, NW), BF16),
             vmem((4, 3, SH, NW), BF16),
             vmem((4, SH, NW), BF16),
-            pltpu.SemaphoreType.REGULAR, dma((8,)), dma, dma((4,)), dma, dma,
+            pltpu.SemaphoreType.REGULAR, dma((4,)), dma, dma((4,)), dma, dma,
             dma, dma((5,)), dma, dma, dma((2,)), dma, dma((4,)),
             dma, dma((4, 4)), dma, dma((4, 3)), dma, dma,
         ],

time: 59.4 us -> 59.4 us (level)
  no operation moved by 1% of the time
where the time goes in v6:
time: 59.4 us; the launch traced here: 59.3 us
  Pallas kernels  57.6 us (97%)
  local copies, waits for them, and re-layouts  1.62 us (3%)
    pallas_call x1, Pallas kernels, on_device(): pl.pallas_call(kernel, out_shape=jax.ShapeDtypeStruct((1, TOK, 2 * NW), B...  57.6 us
    unnamed x1, local copies, waits for them, and re-layouts  1.62 us

profile of v6, /device:TPU:33, one launch (start us, length us, event | category | flops | bytes accessed | tf_op | source)
XLA Modules:
  0.0 59.3 jit_solution(4402102433874313481)
XLA Ops:
  0.0 57.6 %shard_map.82 = bf16[1,128,768]{2,1,0:T(8,128)(2,1)} custom-call(bf16[1,128,1024]{2,1,0:T(8,128)(2,1)} %k_hbm.1, bf16[1,128,1024]{2,1,0:T(8,128)(2,1)} %v_hbm.1, bf16[1,128,1024]{2,1,0:T(8,128)(2,1)} %q_hbm.1, bf16[1,128,1024]{2,1,0:T(8,128)(2,1)} %g_hbm.1, f32[8,128]{1,0:T(8,128)} %bitcast.3, s32[1,128]{1,0:T(1,128)} %docs_hbm.1, f32[1,1024]{1,0:T(1,128)} %gain_hbm.1, ...), custom_call_target="tpu_custom_call" | custom-call | flops 2000000000 | bytes 3145728 | tf_op jit(solution)/shard_map/pallas_call | solution.py:405
  57.6 1.6 %copy.10 = bf16[1,128,768]{2,1,0:T(8,128)(2,1)} copy(bf16[1,128,768]{2,1,0:T(8,128)(2,1)} %shard_map.82) | data formatting | bytes 393216

commit v7 on v6

--- a/solution.py
+++ b/solution.py
@@ -216,7 +216,6 @@
     st_out[256:272, :] = jnp.broadcast_to(last_doc, (16, DH)).astype(BF16)
     send(st_out, st_in, st_sem.at[0], st_sem.at[1], (at_y(1), z, p))
     weights(1, ((0, 3),))
-    relays(1)
     weights(0, ((0, 0), (0, 1), (0, 2), (1, 0), (0, 3), (1, 1)))
 
     base = lax.broadcasted_iota(jnp.int32, (TOK, 4 * TOK), 0)
@@ -264,6 +263,7 @@
     local[6].wait()
     for j in range(4):
         inside(j)
+    relays(1)
     a2a_wait(3)
     arrived(st_in, st_sem.at[1])
     for j in range(4):

time: 59.4 us -> 59.3 us (level)
  no operation moved by 1% of the time
where the time goes in v7:
time: 59.3 us; the launch traced here: 59.2 us
  Pallas kernels  57.6 us (97%)
  local copies, waits for them, and re-layouts  1.62 us (3%)
    pallas_call x1, Pallas kernels, on_device(): pl.pallas_call(kernel, out_shape=jax.ShapeDtypeStruct((1, TOK, 2 * NW), B...  57.6 us
    unnamed x1, local copies, waits for them, and re-layouts  1.62 us

profile of v7, /device:TPU:33, one launch (start us, length us, event | category | flops | bytes accessed | tf_op | source)
XLA Modules:
  0.0 59.2 jit_solution(12625673757267491281)
XLA Ops:
  0.0 57.6 %shard_map.82 = bf16[1,128,768]{2,1,0:T(8,128)(2,1)} custom-call(bf16[1,128,1024]{2,1,0:T(8,128)(2,1)} %k_hbm.1, bf16[1,128,1024]{2,1,0:T(8,128)(2,1)} %v_hbm.1, bf16[1,128,1024]{2,1,0:T(8,128)(2,1)} %q_hbm.1, bf16[1,128,1024]{2,1,0:T(8,128)(2,1)} %g_hbm.1, f32[8,128]{1,0:T(8,128)} %bitcast.3, s32[1,128]{1,0:T(1,128)} %docs_hbm.1, f32[1,1024]{1,0:T(1,128)} %gain_hbm.1, ...), custom_call_target="tpu_custom_call" | custom-call | flops 2000000000 | bytes 3145728 | tf_op jit(solution)/shard_map/pallas_call | solution.py:405
  57.6 1.6 %copy.10 = bf16[1,128,768]{2,1,0:T(8,128)(2,1)} copy(bf16[1,128,768]{2,1,0:T(8,128)(2,1)} %shard_map.82) | data formatting | bytes 393216
